TPU v7x, 256 devices: a whole 4x4x8 slice. The times are simulated.
256 devices in a mesh: frame: 32 (over z_lo, x, core), fsdp: 8 (over y, z_hi).
Axes of the slice: x: 4, y: 4, z: 8 (z_hi: 2, z_lo: 4; z = z_hi * 4 + z_lo), core: 2. Of those that a mesh axis runs over, the one named last changes fastest.
Arguments:
- tokens: bfloat16 [32, 16, 32, 3072], P('frame', 'fsdp'), may hold values from -48 to 48
- frame_time: int32 [32], replicated, may hold values from 0 to 15
- qkv_weight: bfloat16 [3, 3072, 2048], P(None, 'frame', 'fsdp'), may hold values from -0.109375 to 0.109375
- out_weight: bfloat16 [2048, 3072], P('fsdp', 'frame'), may hold values from -2 to 2
- norm_gain: bfloat16 [3072], replicated, may hold values from 0.099609375 to 1.8984375
- conv_weight: bfloat16 [3, 3, 3072], replicated, may hold values from -2 to 2
- up_weight: bfloat16 [3072, 3072], P('frame', 'fsdp'), may hold values from -0.109375 to 0.109375
- down_weight: bfloat16 [3072, 3072], P('fsdp', 'frame'), may hold values from -0.109375 to 0.109375
Outputs:
- layer_out: bfloat16 [32, 16, 32, 3072], P('frame', 'fsdp')
All inputs are finite; a program needn't handle non-finite values.
Results may differ from a plain program's by a relative error of at most 0.019.
The roundings to bfloat16 on the way count: a program that leaves them out, or rounds other values in their place, can miss the bound.
Values may be sent and summed in bfloat16 or wider, within the bound.
A program may use at most 192 MiB of HBM per device.

v0:
```python
import math

import jax
import jax.numpy as jnp
from jax import lax
from jax.sharding import PartitionSpec as P

HEAD = 128


def extended(x, sides, width):
    for axis, dim in sides:
        size, length = (lax.axis_size(axis), x.shape[dim])
        up = [(i, (i + 1) % size) for i in range(size - 1)]
        down = [(j, i) for i, j in up]
        last = lax.slice_in_dim(x, length - width, length, axis=dim)
        initial = lax.slice_in_dim(x, 0, width, axis=dim)
        before = lax.ppermute(last, axis, up)
        after = lax.ppermute(initial, axis, down)
        x = jnp.concatenate([before, x, after], axis=dim)
    return x


def table_lookup(table, positions):
    entries = jnp.arange(table.shape[0], dtype=jnp.int32)
    return jnp.sum(jnp.where(positions[:, None] == entries[None, :], table[None, :], 0), axis=1)


def attend_block(carried, queries, keys, values, visible, factor):
    running_max, running_sum, running_out = carried
    scores = jnp.einsum("qhd,khd->hqk", queries, keys, preferred_element_type=jnp.float32) * factor
    scores = jnp.where(visible[None, None, :], scores, -jnp.inf)
    new_max = jnp.max(scores, axis=-1)
    shifted = jnp.where(new_max == -jnp.inf, 0.0, new_max)
    weights = jnp.exp(scores - shifted[:, :, None])
    decay = jnp.exp(running_max - shifted)
    new_sum = running_sum * decay + jnp.sum(weights, axis=-1)
    update = jnp.einsum(
        "hqk,khd->qhd", weights.astype(jnp.bfloat16), values, preferred_element_type=jnp.float32
    )
    new_out = running_out * decay.T[:, :, None] + update
    return (new_max, new_sum, new_out)


def normalize(residual, norm_gain):
    mean_square = jnp.mean(residual * residual, axis=-1, keepdims=True)
    return (residual * lax.rsqrt(mean_square + 1e-06) * norm_gain.astype(jnp.float32)).astype(
        jnp.bfloat16
    )


def grid_conv(row_padded, conv_weight):
    padded = jnp.pad(row_padded, ((0, 0), (0, 0), (1, 1), (0, 0)))
    height = padded.shape[1] - 2
    breadth = padded.shape[2] - 2
    kernel = conv_weight.astype(jnp.float32)
    result = jnp.zeros((padded.shape[0], height, breadth, padded.shape[3]), jnp.float32)
    for vertical in range(3):
        for lateral in range(3):
            window = padded[:, vertical : vertical + height, lateral : lateral + breadth, :].astype(
                jnp.float32
            )
            result = result + window * kernel[vertical, lateral]
    return result.astype(jnp.bfloat16)


def shards(
    tokens, frame_time, qkv_weight, out_weight, norm_gain, conv_weight, up_weight, down_weight
):
    breadth = tokens.shape[2]
    width = tokens.shape[3]
    frame_grid = lax.all_gather(tokens, "fsdp", axis=1, tiled=True)
    frame_height = frame_grid.shape[1]
    count = frame_height * breadth
    frame_flat = frame_grid.reshape(count, width)
    span = qkv_weight.shape[2]
    heads_here = span // HEAD
    factor = 1.0 / math.sqrt(HEAD)
    part = frame_flat
    projected = jnp.einsum(
        "td,idh->ith",
        part,
        lax.all_gather(qkv_weight, "frame", axis=1, tiled=True),
        preferred_element_type=jnp.float32,
    ).astype(jnp.bfloat16)
    frame_index = jnp.reshape(lax.axis_index("frame"), (1,))
    own_time = table_lookup(frame_time, frame_index)[0]
    queries = projected[0].reshape(count, heads_here, HEAD)
    initial = (
        jnp.full((heads_here, count), -jnp.inf, jnp.float32),
        jnp.zeros((heads_here, count), jnp.float32),
        jnp.zeros((count, heads_here, HEAD), jnp.float32),
    )
    key_block = lax.all_gather(projected[1][None], "frame", axis=0, tiled=True)
    value_block = lax.all_gather(projected[2][None], "frame", axis=0, tiled=True)
    blocks = key_block.shape[0]
    keys = key_block.reshape(blocks * count, heads_here, HEAD)
    values = value_block.reshape(blocks * count, heads_here, HEAD)
    key_frame = jnp.arange(blocks * count, dtype=jnp.int32) // count
    visible = table_lookup(frame_time, key_frame) <= own_time
    result = attend_block(initial, queries, keys, values, visible, factor)
    running_max, running_sum, running_out = result
    attention = (running_out / running_sum.T[:, :, None]).reshape(count, span).astype(jnp.bfloat16)
    head_terms = jnp.dot(
        attention,
        lax.all_gather(out_weight, "frame", axis=1, tiled=True),
        preferred_element_type=jnp.float32,
    )
    summed_rows = lax.psum_scatter(
        head_terms.reshape(1, frame_height, breadth, width).astype(jnp.bfloat16),
        "fsdp",
        scatter_dimension=1,
        tiled=True,
    ).astype(jnp.float32)
    residual = tokens.astype(jnp.float32) + summed_rows
    normed = normalize(residual, norm_gain)
    bordered = extended(normed, (("fsdp", 1),), 1)
    conved = grid_conv(bordered, conv_weight)
    ffn_input = lax.all_gather(conved, "fsdp", axis=1, tiled=True).reshape(count, width)
    part = ffn_input
    pre_hidden = jnp.dot(
        part,
        lax.all_gather(up_weight, "frame", axis=0, tiled=True),
        preferred_element_type=jnp.float32,
    )
    hidden = jax.nn.gelu(pre_hidden).astype(jnp.bfloat16)
    lowered = jnp.dot(
        hidden,
        lax.all_gather(down_weight, "frame", axis=1, tiled=True),
        preferred_element_type=jnp.float32,
    )
    ffn_rows = lax.psum_scatter(
        lowered.reshape(1, frame_height, breadth, width).astype(jnp.bfloat16),
        "fsdp",
        scatter_dimension=1,
        tiled=True,
    ).astype(jnp.float32)
    return (residual + ffn_rows).astype(jnp.bfloat16)


def solution(mesh):
    placed = (
        P("frame", "fsdp", None, None),
        P(),
        P(None, "frame", "fsdp"),
        P("fsdp", "frame"),
        P(),
        P(),
        P("frame", "fsdp"),
        P("fsdp", "frame"),
    )
    return jax.shard_map(
        shards,
        mesh=mesh,
        in_specs=placed,
        out_specs=P("frame", "fsdp", None, None),
        check_vma=False,
    )
```

profile of v0, /device:TPU:1, one launch (start us, length us, event | category | flops | bytes accessed | tf_op | source)
XLA Modules:
  0.0 829.8 jit_solution(13127599059678835889)
XLA Ops:
  6.5 0.7 all-gather.11.cloned.1.call-update
  7.3 0.7 all-gather.9.cloned.1.call-update
  8.0 0.0 all-gather.13.cloned.1.call-start
  8.1 97.2 %all-gather.11.cloned.1.call-done = bf16[1,16,32,3072]{3,2,0,1:T(8,128)(2,1)} async-done(((bf16[1,2,32,3072]{3,2,0,1:T(8,128)(2,1)}), bf16[1,16,32,3072]{3,2,0,1:T(8,128)(2,1)}) %all-gather.11.cloned.1.call-update) | async-done | bytes 3145744 | tf_op jit(solution)/shard_map/all_gather | solution.py:72
  105.2 61.7 %all-gather.9.cloned.1.call-done = bf16[3,3072,256]{2,1,0:T(8,128)(2,1)} async-done(((bf16[3,96,256]{2,1,0:T(8,128)(2,1)}), bf16[3,3072,256]{2,1,0:T(8,128)(2,1)}) %all-gather.9.cloned.1.call-update) | async-done | bytes 4718608 | tf_op jit(solution)/shard_map/all_gather | solution.py:83
  166.9 6.0 fusion.12
  172.9 0.1 fusion.65
  173.0 0.8 copy.26
  173.9 0.0 all-gather.15.cloned.1.call-start
  173.9 0.8 copy.30
  174.8 0.0 all-gather.17.cloned.1.call-start
  174.8 0.5 all-gather.17.cloned.1.call-update
  175.4 0.2 reduce-scatter.3.cloned.1.call-start
  175.6 0.5 select_reduce_fusion
  176.1 0.7 fusion.58
  176.8 0.7 broadcast_compare_fusion
  177.5 64.4 %all-gather.13.cloned.1.call-done = bf16[32,512,256]{2,1,0:T(8,128)(2,1)} async-done(((bf16[1,512,256]{2,1,0:T(8,128)(2,1)}), bf16[32,512,256]{2,1,0:T(8,128)(2,1)}) %all-gather.13.cloned.1.call-update) | async-done | bytes 8388624 | tf_op jit(solution)/shard_map/all_gather | solution.py:94
  241.9 12.5 %reshape.113 = bf16[16384,2,128]{2,1,0:T(2,128)(2,1)} reshape(bf16[32,512,256]{2,1,0:T(8,128)(2,1)} %all-gather.13.cloned.1.call-done) | data formatting | bytes 16777216 | tf_op jit(solution)/shard_map/reshape | solution.py:97
  254.5 28.7 %fusion = (f32[2,512]{1,0:T(2,128)S(1)}, f32[2,512,16384]{2,1,0:T(8,128)}) fusion(pred[16384]{0:T(1024)(128)(4,1)S(1)} %broadcast_compare_fusion, bf16[512,2,128]{0,2,1:T(8,128)(2,1)S(1)} %bitcast.48, bf16[16384,2,128]{2,1,0:T(2,128)(2,1)} %reshape.113), kind=kOutput, calls=%fused_computation.2 | convolution fusion | flops 4345297920 | bytes 75780096 | tf_op jit(solution)/shard_map/qhd,khd->hqk/dot_general | solution.py:31
  283.2 22.5 %fusion.1 = f32[2,512]{1,0:T(2,128)S(1)} fusion(f32[2,512,16384]{2,1,0:T(8,128)} %get-tuple-element.22, f32[2,512]{1,0:T(2,128)S(1)} %compare_select_fusion, pred[16384]{0:T(1024)(128)(4,1)S(1)} %broadcast_compare_fusion), kind=kLoop, calls=%fused_computation.3 | loop fusion | flops 67107840 | bytes 67133440 | tf_op jit(solution)/shard_map/reduce_sum | solution.py:37
  305.8 5.8 all-gather.15.cloned.1.call-done
  311.6 12.5 %reshape.114 = bf16[16384,2,128]{2,1,0:T(2,128)(2,1)} reshape(bf16[32,512,256]{2,1,0:T(8,128)(2,1)} %all-gather.15.cloned.1.call-done) | data formatting | bytes 16777216 | tf_op jit(solution)/shard_map/reshape | solution.py:98
  324.1 27.0 %fusion.33 = bf16[512,2,128]{0,2,1:T(8,128)(2,1)S(1)} fusion(f32[2,512,16384]{2,1,0:T(8,128)} %get-tuple-element.22, f32[2,512]{1,0:T(2,128)S(1)} %compare_select_fusion, pred[16384]{0:T(1024)(128)(4,1)S(1)} %broadcast_compare_fusion, bf16[16384,2,128]{2,1,0:T(2,128)(2,1)} %reshape.114, f32[512,2]{0,1:T(2,128)S(1)} %get-tuple-element.20, ...), kind=kOutput, calls=%fused_computation.30 | convolution fusion | flops 4362469376 | bytes 75788288 | tf_op jit(solution)/shard_map/hqk,khd->qhd/dot_general | solution.py:38
  351.2 0.2 copy.32
  351.4 0.2 convert_element_type.97
  351.6 20.1 %all-gather.17.cloned.1.call-done = bf16[256,3072]{0,1:T(8,128)(2,1)} async-done(((bf16[256,96]{0,1:T(8,128)(2,1)}), bf16[256,3072]{0,1:T(8,128)(2,1)}) %all-gather.17.cloned.1.call-update) | async-done | bytes 1572880 | tf_op jit(solution)/shard_map/all_gather | solution.py:106
  371.7 4.1 fusion.9
  375.8 0.0 all-gather.21.cloned.1.call-start
  375.9 0.7 all-gather.21.cloned.1.call-update
  376.6 0.7 all-gather.23.cloned.1.call-update
  377.3 0.0 all-gather.19.cloned.1.call-start
  377.4 106.2 %reduce-scatter.3.cloned.1.call-done = bf16[1,2,32,3072]{3,2,1,0:T(8,128)(2,1)} async-done(((bf16[1,16,32,3072]{3,2,1,0:T(8,128)(2,1)}), bf16[1,2,32,3072]{3,2,1,0:T(8,128)(2,1)}) %reduce-scatter.3.cloned.1.call-update) | async-done | bytes 393232 | tf_op jit(solution)/shard_map/reduce_scatter | solution.py:109
  483.6 1.2 multiply_reduce_fusion
  484.8 1.2 multiply_convert_fusion
  486.0 1.3 collective-permute-start
  487.3 1.5 collective-permute-start.1
  488.9 0.1 fusion.67
  489.0 1.0 collective-permute-done
  489.9 14.9 %collective-permute-done.1 = bf16[1,1,32,3072]{3,2,1,0:T(8,128)(2,1)S(1)} collective-permute-done((bf16[1,1,32,3072]{3,2,1,0:T(8,128)(2,1)S(1)}, bf16[1,1,32,3072]{3,2,1,0:T(8,128)(2,1)S(1)}, u32[]{:S(2)}, u32[]{:S(2)}) %collective-permute-start.1) | collective-permute-done | bytes 196640 | tf_op jit(solution)/shard_map/ppermute | solution.py:19
  504.8 0.3 fusion.27
  505.1 1.4 fusion.51
  506.6 0.0 reduce-scatter.5.cloned.1.call-start
  506.6 42.9 %all-gather.21.cloned.1.call-done = bf16[3072,384]{1,0:T(8,128)(2,1)} async-done(((bf16[96,384]{1,0:T(8,128)(2,1)}), bf16[3072,384]{1,0:T(8,128)(2,1)}) %all-gather.21.cloned.1.call-update) | async-done | bytes 2359312 | tf_op jit(solution)/shard_map/all_gather | solution.py:123
  549.5 65.3 %all-gather.23.cloned.1.call-done = bf16[384,3072]{0,1:T(8,128)(2,1)} async-done(((bf16[384,96]{0,1:T(8,128)(2,1)}), bf16[384,3072]{0,1:T(8,128)(2,1)}) %all-gather.23.cloned.1.call-update) | async-done | bytes 2359312 | tf_op jit(solution)/shard_map/all_gather | solution.py:129
  614.8 92.9 %all-gather.19.cloned.1.call-done = bf16[1,16,32,3072]{3,2,0,1:T(8,128)(2,1)} async-done(((bf16[1,2,32,3072]{3,2,0,1:T(8,128)(2,1)}), bf16[1,16,32,3072]{3,2,0,1:T(8,128)(2,1)}) %all-gather.19.cloned.1.call-update) | async-done | bytes 3145744 | tf_op jit(solution)/shard_map/all_gather | solution.py:119
  707.7 8.5 %convolution_convert_fusion = bf16[512,3072]{1,0:T(8,128)(2,1)} fusion(bf16[384,3072]{0,1:T(8,128)(2,1)} %all-gather.23.cloned.1.call-done, bf16[512,3072]{1,0:T(8,128)(2,1)} %bitcast.59, bf16[3072,384]{1,0:T(8,128)(2,1)} %all-gather.21.cloned.1.call-done), kind=kOutput, calls=%fused_computation.10 | convolution fusion | flops 2419261440 | bytes 11010048 | tf_op jit(solution)/shard_map/dot_general | solution.py:127
  716.3 104.8 %reduce-scatter.5.cloned.1.call-done = bf16[1,2,32,3072]{3,2,1,0:T(8,128)(2,1)} async-done(((bf16[1,16,32,3072]{3,2,1,0:T(8,128)(2,1)}), bf16[1,2,32,3072]{3,2,1,0:T(8,128)(2,1)}) %reduce-scatter.5.cloned.1.call-update) | async-done | bytes 393232 | tf_op jit(solution)/shard_map/reduce_scatter | solution.py:132
  821.1 1.9 add_convert_fusion
  (24 shorter events, 0.3 us)
Async XLA Ops:
  6.5 98.7 %all-gather.11.cloned.1.call-start = ((), (), s32[]{:S(2)}) async-start(), calls=%async_computation.3 | async-start | bytes 3538944 | tf_op jit(solution)/shard_map/all_gather | solution.py:72
  7.3 159.7 %all-gather.9.cloned.1.call-start = ((), (), s32[]{:S(2)}) async-start(), calls=%async_computation.2 | async-start | bytes 4866048 | tf_op jit(solution)/shard_map/all_gather | solution.py:83
  8.0 233.9 %all-gather.13.cloned.1.call-start = ((), (), s32[]{:S(2)}) async-start(), calls=%async_computation.4 | async-start | bytes 8650752 | tf_op jit(solution)/shard_map/all_gather | solution.py:94
  166.9 8.7 %copy-start.4 = (s32[32]{0:T(128)S(1)}, s32[32]{0:T(128)}, u32[]{:S(2)}) copy-start(s32[32]{0:T(128)} %param.9) | copy-start | bytes 388
  173.9 137.7 %all-gather.15.cloned.1.call-start = ((), (), s32[]{:S(2)}) async-start(), calls=%async_computation.5 | async-start | bytes 8650752 | tf_op jit(solution)/shard_map/all_gather | solution.py:95
  174.8 197.0 %all-gather.17.cloned.1.call-start = ((), (), s32[]{:S(2)}) async-start(), calls=%async_computation.6 | async-start | bytes 1622016 | tf_op jit(solution)/shard_map/all_gather | solution.py:106
  175.4 308.2 %reduce-scatter.3.cloned.1.call-start = ((), (), s32[]{:S(2)}) async-start(), calls=%async_computation.7 | async-start | bytes 3538944 | tf_op jit(solution)/shard_map/reduce_scatter | solution.py:109
  351.2 26.2 %copy-start.3 = (bf16[3072]{0:T(1024)(128)(2,1)S(1)}, bf16[3072]{0:T(1024)(128)(2,1)}, u32[]{:S(2)}) copy-start(bf16[3072]{0:T(1024)(128)(2,1)} %param.12) | copy-start | bytes 18436
  351.2 132.4 %copy-start = (bf16[1,2,32,3072]{3,2,1,0:T(8,128)(2,1)S(1)}, bf16[1,2,32,3072]{3,2,1,0:T(8,128)(2,1)}, u32[]{:S(2)}) copy-start(bf16[1,2,32,3072]{3,2,1,0:T(8,128)(2,1)} %param.8) | copy-start | bytes 1179652
  351.6 137.3 %copy-start.2 = (bf16[3,3,3072]{2,1,0:T(4,128)(2,1)S(1)}, bf16[3,3,3072]{2,1,0:T(4,128)(2,1)}, u32[]{:S(2)}) copy-start(bf16[3,3,3072]{2,1,0:T(4,128)(2,1)} %param.13) | copy-start | bytes 165892
  375.8 173.7 %all-gather.21.cloned.1.call-start = ((), (), s32[]{:S(2)}) async-start(), calls=%async_computation.9 | async-start | bytes 2433024 | tf_op jit(solution)/shard_map/all_gather | solution.py:123
  376.6 238.2 %all-gather.23.cloned.1.call-start = ((), (), s32[]{:S(2)}) async-start(), calls=%async_computation.10 | async-start | bytes 2433024 | tf_op jit(solution)/shard_map/all_gather | solution.py:129
  377.3 330.4 %all-gather.19.cloned.1.call-start = ((), (), s32[]{:S(2)}) async-start(), calls=%async_computation.8 | async-start | bytes 3538944 | tf_op jit(solution)/shard_map/all_gather | solution.py:119
  486.0 3.9 collective-permute-start
  487.3 17.5 %collective-permute-start.1 = (bf16[1,1,32,3072]{3,2,1,0:T(8,128)(2,1)S(1)}, bf16[1,1,32,3072]{3,2,1,0:T(8,128)(2,1)S(1)}, u32[]{:S(2)}, u32[]{:S(2)}) collective-permute-start(bf16[1,1,32,3072]{3,2,1,0:T(8,128)(2,1)S(1)} %get-tuple-element.9), channel_id=1, source_target_pairs={{1,0},{2,1},{3,2},{4,3},{5,4},{6,5},{7,6},{9,8},{10,9},{11,10},{12... | collective-permute-start | bytes 589832 | tf_op jit(solution)/shard_map/ppermute | solution.py:19
  506.6 314.5 %reduce-scatter.5.cloned.1.call-start = ((), (), s32[]{:S(2)}) async-start(), calls=%async_computation.11 | async-start | bytes 3538944 | tf_op jit(solution)/shard_map/reduce_scatter | solution.py:132
  707.7 113.3 %copy-start.1 = (bf16[1,2,32,3072]{3,2,1,0:T(8,128)(2,1)S(1)}, bf16[1,2,32,3072]{3,2,1,0:T(8,128)(2,1)}, u32[]{:S(2)}) copy-start(bf16[1,2,32,3072]{3,2,1,0:T(8,128)(2,1)} %reduce-scatter.3.cloned.1.call-done) | copy-start | bytes 1179652
Sparse Core Ops, SparseCore 0:
  10.0 95.2 all-gather.10
  107.0 59.8 all-gather.8
  174.0 67.8 all-gather.12
  243.6 67.9 all-gather.14
  313.3 58.3 all-gather.16
  376.0 107.6 reduce-scatter.2
  485.6 63.8 all-gather.20
  551.5 63.2 all-gather.22
  617.8 89.9 all-gather.18
  716.4 104.6 reduce-scatter.4
where the time goes:
time: 831 us; the launch traced here: 830 us
  waiting for transfers between devices  681 us (82%)
  matrix products  74.4 us (9%)
  other arithmetic  30.4 us (4%)
  local copies, waits for them, and re-layouts  27.3 us (3%)
  between operations  13.7 us (2%)
    reduce_scatter x1, waiting for transfers between devices, shards(): lax.psum_scatter(head_terms.reshape(1, frame_height, breadth, width).asty...  106 us
    reduce_scatter x1, waiting for transfers between devices, shards(): lax.psum_scatter(lowered.reshape(1, frame_height, breadth, width).astype(...  105 us
    all_gather x1, waiting for transfers between devices, shards(): frame_grid = lax.all_gather(tokens, 'fsdp', axis=1, tiled=True)  97.2 us
    all_gather x1, waiting for transfers between devices, shards(): lax.all_gather(conved, 'fsdp', axis=1, tiled=True).reshape(count, width)  92.9 us
    all_gather x1, waiting for transfers between devices, shards(): lax.all_gather(down_weight, 'frame', axis=1, tiled=True)  65.3 us
    all_gather x1, waiting for transfers between devices, shards(): key_block = lax.all_gather(projected[1][None], 'frame', axis=0, tiled=True)  64.4 us
    all_gather x1, waiting for transfers between devices, shards(): lax.all_gather(qkv_weight, 'frame', axis=1, tiled=True)  61.7 us
    all_gather x1, waiting for transfers between devices, shards(): lax.all_gather(up_weight, 'frame', axis=0, tiled=True)  42.9 us
  transfers between devices with their start and end apart: 12, of which 12 were waited for; matrix products, arithmetic and copies ran while one was open for 13% of the time, Pallas kernels for 0%

commit v1 on v0

v1 whole, which is shorter than its diff:
```python
import functools
import math

import jax
import jax.numpy as jnp
from jax import lax
from jax.experimental import pallas as pl
from jax.experimental.pallas import tpu as pltpu
from jax.sharding import Mesh
from jax.sharding import PartitionSpec as P

HEAD = 128
MESH = pl.DeviceIdType.MESH
BF = jnp.bfloat16
F32 = jnp.float32
AXES = ("zlo", "x", "core", "y", "zhi")
ANY = pl.BlockSpec(memory_space=pl.ANY)
VMEM = pl.BlockSpec(memory_space=pltpu.VMEM)
SMEM = pl.BlockSpec(memory_space=pltpu.SMEM)
SCALE2 = math.log2(math.e) / math.sqrt(HEAD)


def aligned(index, size):
    return pl.ds(pl.multiple_of(index * size, size), size)


class Place:
    def __init__(self):
        self.zlo, self.x, self.core, self.y, self.zhi = (lax.axis_index(a) for a in AXES)
        turn = 1 - 2 * self.core
        self.chip = self.zlo * 4 + self.x
        self.share = 2 * self.y + self.zhi
        self.xf, self.xb, self.xo = (lax.rem(self.x + 4 + k, 4) for k in (turn, -turn, 2))
        self.yf, self.yb, self.yo = (lax.rem(self.y + 4 + k, 4) for k in (turn, -turn, 2))
        self.partner = {"core": 1 - self.core}
        self.far = {"zhi": 1 - self.zhi}


class Copies:
    def __init__(self, send, recv, local):
        self.send, self.recv, self.local = send, recv, local
        self.pushed, self.kept, self.count = [], [], 0

    def push(self, src, dst, device):
        index = self.count
        self.count += 1
        copy = pltpu.make_async_remote_copy(
            src, dst, self.send.at[index], self.recv.at[index], device_id=device, device_id_type=MESH
        )
        copy.start()
        self.pushed.append(copy)
        return index

    def got(self, index, region):
        pltpu.make_async_copy(region, region, self.recv.at[index]).wait()

    def keep(self, src, dst):
        copy = pltpu.make_async_copy(src, dst, self.local.at[len(self.kept)])
        copy.start()
        self.kept.append(copy)
        return copy

    def sent(self):
        for copy in self.pushed:
            copy.wait_send()


def greet(devices):
    barrier = pltpu.get_barrier_semaphore()
    for device in devices:
        pl.semaphore_signal(barrier, inc=1, device_id=device, device_id_type=MESH)
    pl.semaphore_wait(barrier, len(devices))


def x_start(copies, at, region, z):
    mine = region(z * 4 + at.x)
    return (
        copies.push(mine, mine, {"x": at.xf}),
        copies.push(mine, mine, {"x": at.xb}),
    )


def x_forward(copies, at, region, z, started):
    block = region(z * 4 + at.xb)
    copies.got(started[0], block)
    return copies.push(block, block, {"x": at.xf})


def x_rest(copies, at, region, z, started, forwarded):
    copies.got(started[1], region(z * 4 + at.xf))
    copies.got(forwarded, region(z * 4 + at.xo))


def scratch(pushes, locals_):
    return [
        pltpu.SemaphoreType.DMA((pushes,)),
        pltpu.SemaphoreType.DMA((pushes,)),
        pltpu.SemaphoreType.DMA((locals_,)),
    ]


def spread_kernel(tok, wq, wo, tok_all, wq_all, wo_all, send, recv, local):
    at = Place()
    copies = Copies(send, recv, local)
    zs = [lax.rem(at.zlo + k, 4) for k in (1, 3, 2)]
    zfrom = [lax.rem(at.zlo + 4 - k, 4) for k in (1, 3, 2)]
    greet(
        [at.partner, at.far, {"y": at.yf}, {"y": at.yb}, {"x": at.xf}, {"x": at.xb}]
        + [{"zlo": z} for z in zs]
    )

    def piece(share, half):
        return tok_all.at[at.core, share, pl.ds(32 * half, 32)]

    def wq_block(chip):
        return wq_all.at[:, aligned(chip, 192)]

    def wo_block(chip):
        return wo_all.at[:, chip]

    halves = (0, 1)
    source = [tok.at[pl.ds(32 * h, 32)] for h in halves]
    rows = wq_all.at[:, aligned(2 * at.chip + at.core, 96)]
    w_pair = copies.push(wq.at[:, :, aligned(1 - at.core, HEAD)], rows, at.partner)
    w_own = copies.keep(wq.at[:, :, aligned(at.core, HEAD)], rows)
    o_far = copies.push(wo, wo_all.at[at.zhi, at.chip], at.far)
    o_own = copies.keep(wo, wo_all.at[at.zhi, at.chip])
    far = [copies.push(source[h], piece(at.share, h), at.far) for h in halves]
    own_f = [copies.push(source[h], piece(at.share, h), {"y": at.yf}) for h in halves]
    own_b = [copies.push(source[h], piece(at.share, h), {"y": at.yb}) for h in halves]
    t_own = copies.keep(tok, tok_all.at[at.core, at.share])

    partner_rows = wq_all.at[:, aligned(2 * at.chip + 1 - at.core, 96)]
    copies.got(w_pair, partner_rows)
    w_own.wait()
    w_z = [copies.push(wq_block(at.chip), wq_block(at.chip), {"zlo": z}) for z in zs]
    w_x = [x_start(copies, at, wq_block, at.zlo)]
    copies.got(o_far, wo_all.at[1 - at.zhi, at.chip])
    o_own.wait()
    o_z = [copies.push(wo_block(at.chip), wo_block(at.chip), {"zlo": z}) for z in zs]
    o_x = [x_start(copies, at, wo_block, at.zlo)]

    shared = []

    def share_out(share):
        block = tok_all.at[at.core, share]
        shared.append((copies.push(block, block, at.partner), share))

    t_own.wait()
    share_out(at.share)
    back = 2 * at.yb + at.zhi
    ahead = 2 * at.yf + at.zhi
    beyond = 2 * at.yo + at.zhi
    fwd = []
    for h in halves:
        copies.got(own_f[h], piece(back, h))
        fwd.append(copies.push(piece(back, h), piece(back, h), {"y": at.yf}))
    w_f = [x_forward(copies, at, wq_block, at.zlo, w_x[0])]
    o_f = [x_forward(copies, at, wo_block, at.zlo, o_x[0])]
    share_out(back)
    for h in halves:
        copies.got(own_b[h], piece(ahead, h))
    share_out(ahead)
    far_share = 2 * at.y + 1 - at.zhi
    far_f, far_b = [], []
    for h in halves:
        copies.got(far[h], piece(far_share, h))
        far_f.append(copies.push(piece(far_share, h), piece(far_share, h), {"y": at.yf}))
        far_b.append(copies.push(piece(far_share, h), piece(far_share, h), {"y": at.yb}))
    share_out(far_share)
    for k in range(3):
        copies.got(w_z[k], wq_block(zfrom[k] * 4 + at.x))
        w_x.append(x_start(copies, at, wq_block, zfrom[k]))
        copies.got(o_z[k], wo_block(zfrom[k] * 4 + at.x))
        o_x.append(x_start(copies, at, wo_block, zfrom[k]))
    for h in halves:
        copies.got(fwd[h], piece(beyond, h))
    share_out(beyond)
    back, ahead, beyond = back + 1 - 2 * at.zhi, ahead + 1 - 2 * at.zhi, beyond + 1 - 2 * at.zhi
    w_f.append(x_forward(copies, at, wq_block, zfrom[0], w_x[1]))
    o_f.append(x_forward(copies, at, wo_block, zfrom[0], o_x[1]))
    fwd = []
    for h in halves:
        copies.got(far_f[h], piece(back, h))
        fwd.append(copies.push(piece(back, h), piece(back, h), {"y": at.yf}))
    share_out(back)
    for k in (1, 2):
        w_f.append(x_forward(copies, at, wq_block, zfrom[k], w_x[k + 1]))
        o_f.append(x_forward(copies, at, wo_block, zfrom[k], o_x[k + 1]))
    for h in halves:
        copies.got(far_b[h], piece(ahead, h))
    share_out(ahead)
    for h in halves:
        copies.got(fwd[h], piece(beyond, h))
    share_out(beyond)
    for k, z in enumerate([at.zlo] + zfrom):
        x_rest(copies, at, wq_block, z, w_x[k], w_f[k])
        x_rest(copies, at, wo_block, z, o_x[k], o_f[k])
    for index, share in shared:
        copies.got(index, tok_all.at[1 - at.core, share])
    copies.sent()


def attend_kernel(times, qkv, wo, out, wo_all, kv, top, total, mixed, send, recv, local):
    at = Place()
    copies = Copies(send, recv, local)
    zs = [lax.rem(at.zlo + k, 4) for k in (1, 3, 2)]
    zfrom = [lax.rem(at.zlo + 4 - k, 4) for k in (1, 3, 2)]
    greet(
        [at.partner, {"y": at.yf}, {"y": at.yb}, {"x": at.xf}, {"x": at.xb}]
        + [{"zlo": z} for z in zs]
    )

    def kv_block(chip):
        return kv.at[chip]

    def wo_block(y, core):
        return wo_all.at[pl.ds(2 * y, 2), :, core]

    def attend(chip):
        def tile(t, carry):
            rows = aligned(t, 256)
            own_time = times[2 * at.chip + t // 2]
            scores = lax.dot_general(
                qkv[0, rows, :], kv[chip, 0], (((1,), (1,)), ((), ())), preferred_element_type=F32
            )
            seen = [times[2 * chip + j] <= own_time for j in (0, 1)]
            parts = [scores[:, :512], scores[:, 512:]]
            old = top[rows, :1]
            new = old
            for part, see in zip(parts, seen):
                new = jnp.maximum(
                    new, jnp.where(see, jnp.max(part, axis=1, keepdims=True), -1e30)
                )
            decay = jnp.exp2((old - new) * SCALE2)
            weights = [
                jnp.exp2((part - jnp.where(see, new, 1e30)) * SCALE2)
                for part, see in zip(parts, seen)
            ]
            lanes = total[rows, :] * decay
            for part in weights:
                for j in range(4):
                    lanes = lanes + part[:, 128 * j : 128 * j + 128]
            total[rows, :] = lanes
            top[rows, :] = jnp.broadcast_to(new, (256, 128))
            both = jnp.concatenate([part.astype(BF) for part in weights], axis=1)
            mixed[rows, :] = mixed[rows, :] * decay + jnp.dot(
                both, kv[chip, 1], preferred_element_type=F32
            )
            return carry

        lax.fori_loop(0, 4, tile, 0)

    own = qkv.at[pl.ds(1, 2)]
    kv_z = [copies.push(own, kv_block(at.chip), {"zlo": zs[0]})]
    kv_x = [
        (
            copies.push(own, kv_block(at.chip), {"x": at.xf}),
            copies.push(own, kv_block(at.chip), {"x": at.xb}),
        )
    ]
    first_z = copies.pushed[0]
    kv_own = copies.keep(own, kv_block(at.chip))
    wo_f = copies.push(wo, wo_block(at.y, at.core), {"y": at.yf})
    wo_b = copies.push(wo, wo_block(at.y, at.core), {"y": at.yb})
    wo_own = copies.keep(wo, wo_block(at.y, at.core))
    wo_p = [copies.push(wo, wo_block(at.y, at.core), at.partner)]
    top[...] = jnp.full_like(top, -1e30)
    total[...] = jnp.zeros_like(total)
    mixed[...] = jnp.zeros_like(mixed)
    kv_own.wait()
    attend(at.chip)
    z_sends = [first_z]
    order = [at.zlo] + zfrom
    wo_fwd = None
    for k in range(4):
        z = order[k]
        if k > 0:
            attend(z * 4 + at.x)
        forwarded = x_forward(copies, at, kv_block, z, kv_x[k])
        if k == 0:
            copies.pushed[0].wait_send()
            copies.pushed.pop(0)
            kv_z.append(copies.push(own, kv_block(at.chip), {"zlo": zs[1]}))
            second = copies.pushed.pop()
        if k < 3:
            copies.got(kv_z[k], kv_block(zfrom[k] * 4 + at.x))
            kv_x.append(x_start(copies, at, kv_block, zfrom[k]))
        if k == 0:
            second.wait_send()
            kv_z.append(copies.push(own, kv_block(at.chip), {"zlo": zs[2]}))
        attend(z * 4 + at.xb)
        copies.got(kv_x[k][1], kv_block(z * 4 + at.xf))
        attend(z * 4 + at.xf)
        if k == 1:
            block = wo_block(at.yb, at.core)
            copies.got(wo_f, block)
            wo_fwd = copies.push(block, block, {"y": at.yf})
            wo_p.append(copies.push(block, block, at.partner))
        if k == 2:
            block = wo_block(at.yf, at.core)
            copies.got(wo_b, block)
            wo_p.append(copies.push(block, block, at.partner))
        copies.got(forwarded, kv_block(z * 4 + at.xo))
        attend(z * 4 + at.xo)
    out[...] = (mixed[...] / jnp.sum(total[...], axis=1, keepdims=True)).astype(BF)
    block = wo_block(at.yo, at.core)
    copies.got(wo_fwd, block)
    wo_p.append(copies.push(block, block, at.partner))
    wo_own.wait()
    for index, y in zip(wo_p, (at.y, at.yb, at.yf, at.yo)):
        copies.got(index, wo_block(y, 1 - at.core))
    copies.sent()


def rows_kernel(attn, up, down, rows, ud_all, send, recv, local):
    at = Place()
    copies = Copies(send, recv, local)
    deep = at.zhi * 4 + at.zlo
    z_steps = (1, 7, 2, 6, 3, 5, 4)
    zs = [lax.rem(deep + k, 8) for k in z_steps]
    zfrom = [lax.rem(deep + 8 - k, 8) for k in z_steps]
    peers = [(c, z, y) for y in range(4) for z in (1, 0) for c in (0, 1) if (c, z, y) != (0, 0, 0)]

    def peer(c, z, y, sign):
        return (
            lax.rem(at.core + c, 2),
            lax.rem(at.zhi + z, 2),
            lax.rem(at.y + 4 + sign * y, 4),
        )

    def named(place):
        return {"core": place[0], "zhi": place[1], "y": place[2]}

    greet(
        [named(peer(*p, 1)) for p in peers]
        + [{"x": at.xf}, {"x": at.xb}]
        + [{"zhi": z // 4, "zlo": lax.rem(z, 4)} for z in zs[:-1]]
    )

    def head_rows(head):
        return rows.at[:, aligned(head, HEAD)]

    def needed(place):
        core, zhi, y = place
        first = jnp.clip(2 * (2 * y + zhi) - 1, 0, 12)
        return attn.at[core, pl.ds(pl.multiple_of(first * 32, 32), 128)]

    def ud_block(deep_, x):
        return ud_all.at[:, deep_ // 4, lax.rem(deep_, 4) * 4 + x, at.core]

    def ud_lump(deep_, core):
        return ud_all.at[:, deep_ // 4, aligned(lax.rem(deep_, 4), 4), core]

    head = 2 * at.share + at.core
    mine = (at.core, at.zhi, at.y)
    pushes = [copies.push(needed(peer(*p, 1)), head_rows(head), named(peer(*p, 1))) for p in peers]
    kept = copies.keep(needed(mine), head_rows(head))
    both = [
        copies.keep(up, ud_all.at[0, at.zhi, at.chip, at.core]),
        copies.keep(down, ud_all.at[1, at.zhi, at.chip, at.core]),
    ]
    for copy in both:
        copy.wait()
    own = ud_block(deep, at.x)
    ud_z = [copies.push(own, own, {"zhi": z // 4, "zlo": lax.rem(z, 4)}) for z in zs]

    def start(deep_):
        block = ud_block(deep_, at.x)
        return (copies.push(block, block, {"x": at.xf}), copies.push(block, block, {"x": at.xb}))

    started = [start(deep)]
    order = [deep] + zfrom
    lumps = []
    for k in range(8):
        if k < 7:
            copies.got(ud_z[k], ud_block(zfrom[k], at.x))
            started.append(start(zfrom[k]))
        block = ud_block(order[k], at.xb)
        copies.got(started[k][0], block)
        fwd = copies.push(block, block, {"x": at.xf})
        if k > 0:
            finish(k - 1, before)
        before = fwd

        def finish(j, forwarded):
            copies.got(started[j][1], ud_block(order[j], at.xf))
            copies.got(forwarded, ud_block(order[j], at.xo))
            lump = ud_lump(order[j], at.core)
            lumps.append(copies.push(lump, lump, at.partner))

    finish(7, before)
    kept.wait()
    for index, p in zip(pushes, peers):
        core, zhi, y = peer(*p, -1)
        copies.got(index, head_rows(2 * (2 * y + zhi) + core))
    for index, z in zip(lumps, order):
        copies.got(index, ud_lump(z, 1 - at.core))
    copies.sent()


def project_kernel(rows, wo, out):
    acc = jnp.zeros(out.shape, F32)
    for s in range(8):
        acc = acc + lax.dot_general(
            rows[:, 256 * s : 256 * s + 256],
            wo[s],
            (((1,), (1,)), ((), ())),
            preferred_element_type=F32,
        )
    out[...] = acc


def ring_kernel(part, whole, send, recv, local):
    at = Place()
    copies = Copies(send, recv, local)
    greet([{"y": at.yf}, {"y": at.yb}])
    halves = (0, 1)

    def piece(y, h):
        return whole.at[y, pl.ds(32 * h, 32)]

    source = [part.at[pl.ds(32 * h, 32)] for h in halves]
    ahead = [copies.push(source[h], piece(at.y, h), {"y": at.yf}) for h in halves]
    behind = [copies.push(source[h], piece(at.y, h), {"y": at.yb}) for h in halves]
    own = copies.keep(part, whole.at[at.y])
    fwd = []
    for h in halves:
        copies.got(ahead[h], piece(at.yb, h))
        fwd.append(copies.push(piece(at.yb, h), piece(at.yb, h), {"y": at.yf}))
    for h in halves:
        copies.got(behind[h], piece(at.yf, h))
        copies.got(fwd[h], piece(at.yo, h))
    own.wait()
    copies.sent()


def sum_kernel(terms, out, relay, direct, summed, final, send, recv):
    at = Place()
    copies = Copies(send, recv, None)
    greet([{"y": at.yf}, {"y": at.yb}])
    halves = (0, 1)

    def term(y, h):
        return terms.at[y, pl.ds(32 * h, 32)]

    def half(ref, h):
        return ref.at[pl.ds(32 * h, 32)]

    relays = [copies.push(term(at.yo, h), half(relay, h), {"y": at.yf}) for h in halves]
    directs = [copies.push(term(at.yb, h), half(direct, h), {"y": at.yb}) for h in halves]
    finals = []
    for h in halves:
        copies.got(relays[h], half(relay, h))
        rows = pl.ds(32 * h, 32)
        summed[rows, :] = (terms[at.yf, rows, :].astype(F32) + relay[rows, :].astype(F32)).astype(
            BF
        )
        finals.append(copies.push(half(summed, h), half(final, h), {"y": at.yf}))
    for h in halves:
        rows = pl.ds(32 * h, 32)
        copies.got(directs[h], half(direct, h))
        partial = terms[at.y, rows, :].astype(F32) + direct[rows, :].astype(F32)
        copies.got(finals[h], half(final, h))
        out[rows, :] = partial + final[rows, :].astype(F32)
    copies.sent()


def remote(collective_id, megabytes=32):
    return pltpu.CompilerParams(
        collective_id=collective_id, has_side_effects=True, vmem_limit_bytes=megabytes << 20
    )


def shape(*dims, dtype=BF):
    return jax.ShapeDtypeStruct(dims, dtype)


def grid_conv(window, conv_weight):
    padded = jnp.pad(window, ((0, 0), (1, 1), (0, 0)))
    kernel = conv_weight.astype(F32)
    result = jnp.zeros((2, 32, window.shape[2]), F32)
    for vertical in range(3):
        for lateral in range(3):
            part = padded[vertical : vertical + 2, lateral : lateral + 32, :].astype(F32)
            result = result + part * kernel[vertical, lateral]
    return result.astype(BF)


def shards(
    tokens, frame_time, qkv_weight, out_weight, norm_gain, conv_weight, up_weight, down_weight
):
    width = tokens.shape[3]
    core, y, zhi = (lax.axis_index(a) for a in ("core", "y", "zhi"))
    share = 2 * y + zhi
    tok_all, wq_all, wo_part = pl.pallas_call(
        spread_kernel,
        out_shape=(shape(2, 8, 64, width), shape(3, width, HEAD), shape(2, 16, 96, 256)),
        in_specs=[ANY] * 3,
        out_specs=(ANY,) * 3,
        scratch_shapes=scratch(64, 4),
        compiler_params=remote(1),
    )(tokens.reshape(64, width), qkv_weight, out_weight.T)
    qkv = jnp.einsum(
        "td,idh->ith", tok_all.reshape(1024, width), wq_all, preferred_element_type=F32
    ).astype(BF)
    attn, wo_all = pl.pallas_call(
        attend_kernel,
        out_shape=(shape(1024, HEAD), shape(8, 16, 2, 96, 256)),
        in_specs=[SMEM, VMEM, ANY],
        out_specs=(VMEM, ANY),
        scratch_shapes=[
            pltpu.VMEM((16, 2, 1024, HEAD), BF),
            pltpu.VMEM((1024, HEAD), F32),
            pltpu.VMEM((1024, HEAD), F32),
            pltpu.VMEM((1024, HEAD), F32),
        ]
        + scratch(24, 2),
        compiler_params=remote(2, 40),
    )(frame_time, qkv, wo_part)
    rows, ud_all = pl.pallas_call(
        rows_kernel,
        out_shape=(shape(128, 16 * HEAD), shape(2, 2, 16, 2, 96, 384)),
        in_specs=[ANY] * 3,
        out_specs=(ANY,) * 2,
        scratch_shapes=scratch(64, 3),
        compiler_params=remote(3),
    )(attn.reshape(2, 512, HEAD), up_weight, down_weight.T)
    projected = pl.pallas_call(
        project_kernel,
        grid=(12,),
        out_shape=shape(128, width, dtype=F32),
        in_specs=[
            pl.BlockSpec((128, 16 * HEAD), lambda n: (0, 0)),
            pl.BlockSpec((8, 256, 256), lambda n: (0, n, 0)),
        ],
        out_specs=pl.BlockSpec((128, 256), lambda n: (0, n)),
    )(rows, wo_all.reshape(8, width, 256))
    first = jnp.clip(2 * share - 1, 0, 12)
    frame = lax.dynamic_index_in_dim(tok_all, core, 0, keepdims=False).reshape(16, 32, width)
    near = lax.dynamic_slice_in_dim(frame, first, 4, 0)
    residual = near.astype(F32) + projected.reshape(4, 32, width)
    mean_square = jnp.mean(residual * residual, axis=-1, keepdims=True)
    normed = (residual * lax.rsqrt(mean_square + 1e-06) * norm_gain.astype(F32)).astype(BF)
    shift = 2 * share - 1 - first
    window = lax.dynamic_slice_in_dim(
        jnp.pad(normed, ((1, 1), (0, 0), (0, 0))), 1 + shift, 4, 0
    )
    own_residual = lax.dynamic_slice_in_dim(residual, 1 + shift, 2, 0)
    conved = grid_conv(window, conv_weight).reshape(64, width)
    gathered = pl.pallas_call(
        ring_kernel,
        out_shape=shape(4, 64, width),
        in_specs=[ANY],
        out_specs=ANY,
        scratch_shapes=scratch(8, 1),
        compiler_params=remote(4),
    )(conved).reshape(256, width)
    up_all = ud_all[0].reshape(2, width, 384)
    down_all = ud_all[1].reshape(2, width, 384)
    lowered = jnp.zeros((256, width), F32)
    for z in range(2):
        hidden = jax.nn.gelu(jnp.dot(gathered, up_all[z], preferred_element_type=F32)).astype(BF)
        lowered = lowered + lax.dot_general(
            hidden, down_all[z], (((1,), (1,)), ((), ())), preferred_element_type=F32
        )
    summed = pl.pallas_call(
        sum_kernel,
        out_shape=shape(64, width, dtype=F32),
        in_specs=[VMEM],
        out_specs=VMEM,
        scratch_shapes=[pltpu.VMEM((64, width), BF)] * 4 + scratch(8, 1)[:2],
        compiler_params=remote(5),
    )(lowered.astype(BF).reshape(4, 64, width))
    return (own_residual + summed.reshape(2, 32, width)).astype(BF)[None]


def solution(mesh):
    fine = Mesh(mesh.devices.reshape(4, 4, 2, 4, 2), AXES)
    frame, fsdp = ("zlo", "x", "core"), ("y", "zhi")
    placed = (
        P(frame, fsdp, None, None),
        P(),
        P(None, frame, fsdp),
        P(fsdp, frame),
        P(),
        P(),
        P(frame, fsdp),
        P(fsdp, frame),
    )
    return jax.shard_map(
        shards,
        mesh=fine,
        in_specs=placed,
        out_specs=P(frame, fsdp, None, None),
        check_vma=False,
    )
```

time: 831 us -> 320 us (0.39)
  waiting for transfers between devices: 681 us -> 0 us
  Pallas kernels: 0 us -> 286 us
  matrix products: 74.4 us -> 14.6 us
  other arithmetic: 30.4 us -> 4.48 us
  local copies, waits for them, and re-layouts: 27.3 us -> 13.6 us
  between operations: 13.7 us -> 0.17 us
    all_gather x8 -> x0, waiting for transfers between devices: 450 us -> none  [the longest x1 97.2 us: shards(): frame_grid = lax.all_gather(tokens, 'fsdp', axis=1, tiled=True)]
    pallas_call x0 -> x6, Pallas kernels: none -> 286 us  [the longest x1 98.8 us: shards(): pl.pallas_call(attend_kernel, out_shape=(shape(1024, HEAD), shape(8, 16,...]
    reduce_scatter x2 -> x0, waiting for transfers between devices: 211 us -> none  [the longest x1 106 us: shards(): lax.psum_scatter(head_terms.reshape(1, frame_height, breadth, width).asty...]
    dot_general x5 -> x3, matrix products: 74.4 us -> 14.6 us  [the longest x2 11.2 us: shards(): lax.dot_general(hidden, down_all[z], (((1,), (1,)), ((), ())), preferred_...]
    reshape x2 -> x0, local copies, waits for them, and re-layouts: 25.1 us -> none  [the longest x1 12.5 us: shards(): keys = key_block.reshape(blocks * count, heads_here, HEAD)]
    reduce_sum x4 -> x1, other arithmetic: 24.9 us -> 1.86 us  [shards(): mean_square = jnp.mean(residual * residual, axis=-1, keepdims=True)]
    ppermute x2 -> x0, waiting for transfers between devices: 15.9 us -> none  [the longest x1 14.9 us: extended(): after = lax.ppermute(initial, axis, down)]
  transfers between devices with their start and end apart: 12 -> 0, of which waited for: 12 -> 0; matrix products, arithmetic and copies ran while one was open for 13% -> 0% of each run, Pallas kernels for 0% -> 0%
where the time goes in v1:
time: 320 us; the launch traced here: 318 us
  Pallas kernels  286 us (89%)
  matrix products  14.6 us (5%)
  local copies, waits for them, and re-layouts  13.6 us (4%)
  other arithmetic  4.48 us (1%)
    pallas_call x1, Pallas kernels, shards(): pl.pallas_call(attend_kernel, out_shape=(shape(1024, HEAD), shape(8, 16,...  98.8 us
    pallas_call x1, Pallas kernels, shards(): pl.pallas_call(rows_kernel, out_shape=(shape(128, 16 * HEAD), shape(2, 2,...  76.5 us
    pallas_call x1, Pallas kernels, shards(): pl.pallas_call(spread_kernel, out_shape=(shape(2, 8, 64, width), shape(3,...  64.5 us
    pallas_call x1, Pallas kernels, shards(): pl.pallas_call(sum_kernel, out_shape=shape(64, width, dtype=F32), in_spec...  16.9 us
    pallas_call x1, Pallas kernels, shards(): pl.pallas_call(ring_kernel, out_shape=shape(4, 64, width), in_specs=[ANY]...  16.5 us
    pallas_call x1, Pallas kernels, shards(): pl.pallas_call(project_kernel, grid=(12,), out_shape=shape(128, width, dt...  12.4 us
    dot_general x2, matrix products, shards(): lax.dot_general(hidden, down_all[z], (((1,), (1,)), ((), ())), preferred_...  11.2 us
    unnamed x22, local copies, waits for them, and re-layouts  8.31 us

profile of v1, /device:TPU:1, one launch (start us, length us, event | category | flops | bytes accessed | tf_op | source)
XLA Modules:
  0.0 318.5 jit_solution(997048580514716546)
XLA Ops:
  0.0 0.7 convert_element_type.66
  0.7 1.1 fusion.39
  1.7 0.0 copy-start.3
  1.8 1.0 copy-done.3
  2.7 0.0 copy-start.4
  2.8 0.9 copy-done.4
  3.7 0.0 copy-start.7
  3.7 0.8 copy-done.7
  4.5 64.5 %shard_map.82 = (bf16[2,8,64,3072]{3,2,1,0:T(8,128)(2,1)S(1)}, bf16[3,3072,128]{2,1,0:T(8,128)(2,1)S(1)}, bf16[2,16,96,256]{3,2,1,0:T(8,128)(2,1)S(1)}) custom-call(bf16[64,3072]{1,0:T(8,128)(2,1)S(1)} %bitcast.45, bf16[3,96,256]{2,1,0:T(8,128)(2,1)S(1)} %copy-done.4, bf16[96,256]{1,0:T(8,128)(2,1)S(1)} %bitcast.48), custom_call_target="tpu_custom_call" | custom-call | tf_op jit(solution)/shard_map/pallas_call | solution.py:496
  68.9 3.4 %fusion.1.qkv = bf16[3,1024,128]{2,1,0:T(8,128)(2,1)S(1)} fusion(bf16[1024,3072,1]{1,0,2:T(8,128)(2,1)S(1)} %bitcast.43, bf16[3,3072,128]{2,1,0:T(8,128)(2,1)S(1)} %get-tuple-element.13), kind=kOutput, calls=%fused_computation.10 | convolution fusion | flops 2416312320 | bytes 9437184 | tf_op jit(solution)/shard_map/td,idh->ith/dot_general | solution.py:504
  72.3 0.0 copy-start.8
  72.4 0.3 constant_dynamic-slice_fusion
  72.7 0.0 copy-start.5
  72.7 0.0 copy-start.6
  72.7 0.3 copy-done.8
  73.0 98.8 %shard_map.83 = (bf16[1024,128]{1,0:T(8,128)(2,1)S(1)}, bf16[8,16,2,96,256]{4,3,2,1,0:T(8,128)(2,1)}) custom-call(s32[32]{0:T(128)S(1)} %copy-done.8, bf16[3,1024,128]{2,1,0:T(8,128)(2,1)S(1)} %fusion.1.qkv, bf16[2,16,96,256]{3,2,1,0:T(8,128)(2,1)S(1)} %get-tuple-element.14.wo), custom_call_target="tpu_custom_call" | custom-call | tf_op jit(solution)/shard_map/pallas_call | solution.py:507
  171.8 0.0 copy-done.5
  171.9 0.0 copy-done.6
  171.9 76.5 %shard_map.84 = (bf16[128,2048]{1,0:T(8,128)(2,1)S(1)}, bf16[2,2,16,2,96,384]{5,4,3,2,1,0:T(8,128)(2,1)S(1)}) custom-call(bf16[2,512,128]{2,1,0:T(8,128)(2,1)S(1)} %bitcast.46, bf16[96,384]{1,0:T(8,128)(2,1)S(1)} %copy-done.5, bf16[96,384]{1,0:T(8,128)(2,1)S(1)} %bitcast.47), custom_call_target="tpu_custom_call" | custom-call | tf_op jit(solution)/shard_map/pallas_call | solution.py:521
  248.4 0.0 copy-start
  248.4 3.6 %copy-done = bf16[2,2,16,2,96,384]{5,4,3,2,1,0:T(8,128)(2,1)} copy-done((bf16[2,2,16,2,96,384]{5,4,3,2,1,0:T(8,128)(2,1)}, bf16[2,2,16,2,96,384]{5,4,3,2,1,0:T(8,128)(2,1)S(1)}, u32[]{:S(2)}) %copy-start) | copy-done | bytes 9437208
  251.9 0.0 copy-start.2
  251.9 0.8 copy-done.2
  252.7 12.4 %shard_map.85 = f32[128,3072]{1,0:T(8,128)} custom-call(bf16[128,2048]{1,0:T(8,128)(2,1)} %copy-done.2, bf16[8,3072,256]{2,1,0:T(8,128)(2,1)} %bitcast.49), custom_call_target="tpu_custom_call" | custom-call | tf_op jit(solution)/shard_map/pallas_call | solution.py:529
  265.1 0.0 copy-start.1
  265.1 1.9 multiply_reduce_fusion
  267.0 0.0 copy-start.9
  267.0 0.2 multiply_convert_fusion
  267.2 0.9 copy-done.9
  268.2 0.1 pad_dynamic-slice_fusion.3
  268.3 0.9 add_convert_fusion.1
  269.2 16.5 %shard_map.86 = bf16[4,64,3072]{2,1,0:T(8,128)(2,1)S(1)} custom-call(bf16[64,3072]{1,0:T(8,128)(2,1)S(1)} %bitcast.44), custom_call_target="tpu_custom_call" | custom-call | tf_op jit(solution)/shard_map/pallas_call | solution.py:551
  285.7 0.0 copy-done.1
  285.7 3.8 %fusion.38 = (bf16[1,1,16,2,96,384]{5,4,3,2,1,0:T(8,128)(2,1)}, bf16[1,1,16,2,96,384]{5,4,3,2,1,0:T(8,128)(2,1)}, bf16[1,1,16,2,96,384]{5,4,3,2,1,0:T(8,128)(2,1)}, bf16[1,1,16,2,96,384]{5,4,3,2,1,0:T(8,128)(2,1)}) fusion(bf16[2,2,16,2,96,384]{5,4,3,2,1,0:T(8,128)(2,1)S(1)} %copy-done.1), kind=kLoop, calls=%fused_computation.57 | loop fusion | bytes 18874368 | tf_op jit(solution)/shard_map/slice | solution.py:563
  289.5 5.9 %fusion.20 = f32[256,3072]{1,0:T(8,128)} fusion(bf16[3072,384]{1,0:T(8,128)(2,1)} %bitcast.52, bf16[256,3072]{1,0:T(8,128)(2,1)S(1)} %bitcast.39, bf16[3072,384]{1,0:T(8,128)(2,1)} %bitcast.53), kind=kOutput, calls=%fused_computation.38 | convolution fusion | flops 1208844288 | bytes 9437184 | tf_op jit(solution)/shard_map/dot_general | solution.py:564
  295.4 5.2 %fusion = bf16[256,3072]{1,0:T(8,128)(2,1)S(1)} fusion(f32[256,3072]{1,0:T(8,128)} %fusion.20, bf16[3072,384]{1,0:T(8,128)(2,1)} %bitcast.51, bf16[256,3072]{1,0:T(8,128)(2,1)S(1)} %bitcast.40, bf16[3072,384]{1,0:T(8,128)(2,1)} %bitcast.50), kind=kOutput, calls=%fused_computation.1 | convolution fusion | flops 1210417152 | bytes 11010048 | tf_op jit(solution)/shard_map/dot_general | solution.py:564
  300.7 0.0 copy-start.10
  300.7 16.9 %shard_map.87 = f32[64,3072]{1,0:T(8,128)S(1)} custom-call(bf16[4,64,3072]{2,1,0:T(8,128)(2,1)S(1)} %bitcast.41), custom_call_target="tpu_custom_call" | custom-call | tf_op jit(solution)/shard_map/pallas_call | solution.py:567
  317.6 0.0 copy-done.10
  317.6 0.8 fusion.18
  (1 shorter events, 0.0 us)
Async XLA Ops:
  1.7 1.0 copy-start.3
  2.7 0.9 copy-start.4
  3.7 0.8 copy-start.7
  72.3 0.7 copy-start.8
  72.7 99.2 %copy-start.5 = (bf16[96,384]{1,0:T(8,128)(2,1)S(1)}, bf16[96,384]{1,0:T(8,128)(2,1)}, u32[]{:S(2)}) copy-start(bf16[96,384]{1,0:T(8,128)(2,1)} %up.1) | copy-start | bytes 221188
  72.7 99.2 %copy-start.6 = (bf16[384,96]{0,1:T(8,128)(2,1)S(1)}, bf16[384,96]{0,1:T(8,128)(2,1)}, u32[]{:S(2)}) copy-start(bf16[384,96]{0,1:T(8,128)(2,1)} %param.15) | copy-start | bytes 221188
  248.4 3.6 %copy-start = (bf16[2,2,16,2,96,384]{5,4,3,2,1,0:T(8,128)(2,1)}, bf16[2,2,16,2,96,384]{5,4,3,2,1,0:T(8,128)(2,1)S(1)}, u32[]{:S(2)}) copy-start(bf16[2,2,16,2,96,384]{5,4,3,2,1,0:T(8,128)(2,1)S(1)} %get-tuple-element.18) | copy-start | bytes 28311556
  251.9 0.8 copy-start.2
  265.1 20.5 %copy-start.1 = (bf16[2,2,16,2,96,384]{5,4,3,2,1,0:T(8,128)(2,1)S(1)}, bf16[2,2,16,2,96,384]{5,4,3,2,1,0:T(8,128)(2,1)}, u32[]{:S(2)}) copy-start(bf16[2,2,16,2,96,384]{5,4,3,2,1,0:T(8,128)(2,1)} %copy-done) | copy-start | bytes 28311556
  267.0 1.2 copy-start.9
  300.7 16.9 %copy-start.10 = (f32[4,32,3072]{2,1,0:T(8,128)S(1)}, f32[4,32,3072]{2,1,0:T(8,128)}, u32[]{:S(2)}) copy-start(f32[4,32,3072]{2,1,0:T(8,128)} %copy-done.9) | copy-start | bytes 4718596

commit v2 on v1

--- a/solution.py
+++ b/solution.py
@@ -1,4 +1,3 @@
-import functools
 import math
 
 import jax
@@ -218,9 +217,9 @@
         return wo_all.at[pl.ds(2 * y, 2), :, core]
 
     def attend(chip):
-        def tile(t, carry):
-            rows = aligned(t, 256)
-            own_time = times[2 * at.chip + t // 2]
+        for t in range(2):
+            rows = slice(512 * t, 512 * t + 512)
+            own_time = times[2 * at.chip + t]
             scores = lax.dot_general(
                 qkv[0, rows, :], kv[chip, 0], (((1,), (1,)), ((), ())), preferred_element_type=F32
             )
@@ -242,14 +241,11 @@
                 for j in range(4):
                     lanes = lanes + part[:, 128 * j : 128 * j + 128]
             total[rows, :] = lanes
-            top[rows, :] = jnp.broadcast_to(new, (256, 128))
+            top[rows, :] = jnp.broadcast_to(new, (512, 128))
             both = jnp.concatenate([part.astype(BF) for part in weights], axis=1)
             mixed[rows, :] = mixed[rows, :] * decay + jnp.dot(
                 both, kv[chip, 1], preferred_element_type=F32
             )
-            return carry
-
-        lax.fori_loop(0, 4, tile, 0)
 
     own = qkv.at[pl.ds(1, 2)]
     kv_z = [copies.push(own, kv_block(at.chip), {"zlo": zs[0]})]
@@ -259,7 +255,6 @@
             copies.push(own, kv_block(at.chip), {"x": at.xb}),
         )
     ]
-    first_z = copies.pushed[0]
     kv_own = copies.keep(own, kv_block(at.chip))
     wo_f = copies.push(wo, wo_block(at.y, at.core), {"y": at.yf})
     wo_b = copies.push(wo, wo_block(at.y, at.core), {"y": at.yb})
@@ -270,7 +265,6 @@
     mixed[...] = jnp.zeros_like(mixed)
     kv_own.wait()
     attend(at.chip)
-    z_sends = [first_z]
     order = [at.zlo] + zfrom
     wo_fwd = None
     for k in range(4):
@@ -313,14 +307,40 @@
     copies.sent()
 
 
-def rows_kernel(attn, up, down, rows, ud_all, send, recv, local):
+def layer_kernel(
+    attn,
+    up,
+    down,
+    wo,
+    tok,
+    gain,
+    conv,
+    out,
+    wo_here,
+    rows,
+    near,
+    residual,
+    window,
+    gathered,
+    ud,
+    hidden,
+    terms,
+    relay,
+    direct,
+    summed,
+    final,
+    send,
+    recv,
+    local,
+):
     at = Place()
     copies = Copies(send, recv, local)
+    width = out.shape[1]
     deep = at.zhi * 4 + at.zlo
     z_steps = (1, 7, 2, 6, 3, 5, 4)
     zs = [lax.rem(deep + k, 8) for k in z_steps]
-    zfrom = [lax.rem(deep + 8 - k, 8) for k in z_steps]
-    peers = [(c, z, y) for y in range(4) for z in (1, 0) for c in (0, 1) if (c, z, y) != (0, 0, 0)]
+    order = [deep] + [lax.rem(deep + 8 - k, 8) for k in z_steps]
+    peers = [(c, z, y) for z in (1, 0) for y in range(4) for c in (0, 1) if (c, z, y) != (0, 0, 0)]
 
     def peer(c, z, y, sign):
         return (
@@ -332,137 +352,211 @@
     def named(place):
         return {"core": place[0], "zhi": place[1], "y": place[2]}
 
+    def depth(z):
+        return {"zhi": z // 4, "zlo": lax.rem(z, 4)}
+
     greet(
         [named(peer(*p, 1)) for p in peers]
         + [{"x": at.xf}, {"x": at.xb}]
-        + [{"zhi": z // 4, "zlo": lax.rem(z, 4)} for z in zs[:-1]]
+        + [depth(z) for z in zs[:-1]]
     )
 
     def head_rows(head):
         return rows.at[:, aligned(head, HEAD)]
 
+    def first_row(share):
+        return jnp.clip(2 * share - 1, 0, 12)
+
     def needed(place):
         core, zhi, y = place
-        first = jnp.clip(2 * (2 * y + zhi) - 1, 0, 12)
-        return attn.at[core, pl.ds(pl.multiple_of(first * 32, 32), 128)]
-
-    def ud_block(deep_, x):
-        return ud_all.at[:, deep_ // 4, lax.rem(deep_, 4) * 4 + x, at.core]
-
-    def ud_lump(deep_, core):
-        return ud_all.at[:, deep_ // 4, aligned(lax.rem(deep_, 4), 4), core]
+        return attn.at[core, pl.ds(pl.multiple_of(first_row(2 * y + zhi) * 32, 32), 128)]
+
+    def ud_block(z, x):
+        return ud.at[:, lax.rem(z, 4) * 4 + x, at.core, :, aligned(z // 4, 384)]
+
+    def ud_lump(z, core):
+        return ud.at[:, aligned(lax.rem(z, 4), 4), core, :, aligned(z // 4, 384)]
 
     head = 2 * at.share + at.core
-    mine = (at.core, at.zhi, at.y)
+    first = first_row(at.share)
+    own_ud = [
+        copies.keep(ref, ud.at[i, at.chip, at.core, :, aligned(at.zhi, 384)])
+        for i, ref in enumerate((up, down))
+    ]
     pushes = [copies.push(needed(peer(*p, 1)), head_rows(head), named(peer(*p, 1))) for p in peers]
-    kept = copies.keep(needed(mine), head_rows(head))
-    both = [
-        copies.keep(up, ud_all.at[0, at.zhi, at.chip, at.core]),
-        copies.keep(down, ud_all.at[1, at.zhi, at.chip, at.core]),
-    ]
-    for copy in both:
+    kept = copies.keep(needed((at.core, at.zhi, at.y)), head_rows(head))
+    wo_copy = copies.keep(wo, wo_here)
+    near_copy = copies.keep(
+        tok.at[at.core, pl.ds(pl.multiple_of(first * 32, 32), 128)], near
+    )
+    for copy in own_ud:
         copy.wait()
-    own = ud_block(deep, at.x)
-    ud_z = [copies.push(own, own, {"zhi": z // 4, "zlo": lax.rem(z, 4)}) for z in zs]
-
-    def start(deep_):
-        block = ud_block(deep_, at.x)
+
+    def z_push(k):
+        block = ud_block(deep, at.x)
+        return copies.push(block, block, depth(zs[k]))
+
+    def x_push(z):
+        block = ud_block(z, at.x)
         return (copies.push(block, block, {"x": at.xf}), copies.push(block, block, {"x": at.xb}))
 
-    started = [start(deep)]
-    order = [deep] + zfrom
-    lumps = []
-    for k in range(8):
-        if k < 7:
-            copies.got(ud_z[k], ud_block(zfrom[k], at.x))
-            started.append(start(zfrom[k]))
+    along_z = [z_push(k) for k in (0, 1)]
+    opened, forwarded, lumps = [x_push(deep)], [], []
+
+    def open_group(k):
+        copies.got(along_z[k - 1], ud_block(order[k], at.x))
+        opened.append(x_push(order[k]))
+
+    def forward_group(k):
         block = ud_block(order[k], at.xb)
-        copies.got(started[k][0], block)
-        fwd = copies.push(block, block, {"x": at.xf})
-        if k > 0:
-            finish(k - 1, before)
-        before = fwd
-
-        def finish(j, forwarded):
-            copies.got(started[j][1], ud_block(order[j], at.xf))
-            copies.got(forwarded, ud_block(order[j], at.xo))
-            lump = ud_lump(order[j], at.core)
-            lumps.append(copies.push(lump, lump, at.partner))
-
-    finish(7, before)
+        copies.got(opened[k][0], block)
+        forwarded.append(copies.push(block, block, {"x": at.xf}))
+
+    def close_group(k):
+        copies.got(opened[k][1], ud_block(order[k], at.xf))
+        copies.got(forwarded[k], ud_block(order[k], at.xo))
+        lump = ud_lump(order[k], at.core)
+        lumps.append(copies.push(lump, lump, at.partner))
+
+    shift = 2 * at.share - 1 - first
+    for r in (1, 4):
+        window[r] = jnp.zeros(window.shape[1:], F32)
+    near_copy.wait()
+    wo_copy.wait()
     kept.wait()
     for index, p in zip(pushes, peers):
         core, zhi, y = peer(*p, -1)
         copies.got(index, head_rows(2 * (2 * y + zhi) + core))
+    along_z.extend(z_push(k) for k in range(2, 7))
+    open_group(1)
+    open_group(2)
+    forward_group(0)
+
+    def project(n, carry):
+        columns = aligned(n, 256)
+        acc = near[:, columns].astype(F32)
+        for s in range(8):
+            acc = acc + lax.dot_general(
+                rows[:, 256 * s : 256 * s + 256],
+                wo_here[s, columns, :],
+                (((1,), (1,)), ((), ())),
+                preferred_element_type=F32,
+            )
+        residual[:, columns] = acc
+        return carry
+
+    lax.fori_loop(0, 12, project, 0)
+    forward_group(1)
+    open_group(3)
+    open_group(4)
+    for r in range(4):
+        row = residual[32 * r : 32 * r + 32, :]
+        mean_square = jnp.mean(row * row, axis=1, keepdims=True)
+        normed = row * lax.rsqrt(mean_square + 1e-06) * gain[...].astype(F32)
+        window[1 + r - shift] = normed.astype(BF).astype(F32)
+    close_group(0)
+    forward_group(2)
+    line = lax.broadcasted_iota(jnp.int32, (32, 512), 0)
+
+    def convolve(j):
+        def tile(n, carry):
+            columns = aligned(n, 512)
+            sums = [jnp.zeros((32, 512), F32)] * 3
+            for a in range(3):
+                taps = conv[a, :, columns].astype(F32)
+                values = window[1 + j + a, :, columns]
+                for b in range(3):
+                    sums[b] = sums[b] + values * taps[b : b + 1, :]
+            before = jnp.where(line == 0, 0.0, pltpu.roll(sums[0], 1, 0))
+            after = jnp.where(line == 31, 0.0, pltpu.roll(sums[2], 31, 0))
+            gathered[aligned(2 * at.y + j, 32), columns] = (before + sums[1] + after).astype(BF)
+            return carry
+
+        lax.fori_loop(0, width // 512, tile, 0)
+
+    def token_piece(y, h):
+        return gathered.at[aligned(2 * y + h, 32)]
+
+    ahead, behind = [], []
+    for h in (0, 1):
+        convolve(h)
+        piece = token_piece(at.y, h)
+        ahead.append(copies.push(piece, piece, {"y": at.yf}))
+        behind.append(copies.push(piece, piece, {"y": at.yb}))
+    open_group(5)
+    open_group(6)
+    close_group(1)
+    forward_group(3)
+    token_fwd = []
+    for h in (0, 1):
+        piece = token_piece(at.yb, h)
+        copies.got(ahead[h], piece)
+        token_fwd.append(copies.push(piece, piece, {"y": at.yf}))
+    open_group(7)
+    close_group(2)
+    for k in (4, 5, 6, 7):
+        forward_group(k)
+        close_group(k - 1)
+    close_group(7)
+    for h in (0, 1):
+        copies.got(behind[h], token_piece(at.yf, h))
+        copies.got(token_fwd[h], token_piece(at.yo, h))
     for index, z in zip(lumps, order):
         copies.got(index, ud_lump(z, 1 - at.core))
-    copies.sent()
-
-
-def project_kernel(rows, wo, out):
-    acc = jnp.zeros(out.shape, F32)
-    for s in range(8):
-        acc = acc + lax.dot_general(
-            rows[:, 256 * s : 256 * s + 256],
-            wo[s],
+
+    for n in range(3):
+        columns = slice(256 * n, 256 * n + 256)
+        value = jnp.dot(
+            gathered[...],
+            ud[0, :, :, :, columns].reshape(width, 256),
+            preferred_element_type=F32,
+        )
+        hidden[:, columns] = jax.nn.gelu(value).astype(BF)
+
+    chunk = width // 4
+
+    def columns_of(q):
+        return slice(chunk * q, chunk * q + chunk)
+
+    def term(y, q):
+        return terms.at[aligned(y, 64), pl.ds(chunk * q, chunk)]
+
+    def strip(ref, q):
+        return ref.at[:, pl.ds(chunk * q, chunk)]
+
+    relays, directs, finals = [], [], []
+
+    def pass_on(q):
+        copies.got(relays[q], strip(relay, q))
+        columns = columns_of(q)
+        summed[:, columns] = (
+            terms[aligned(at.yf, 64), columns].astype(F32) + relay[:, columns].astype(F32)
+        ).astype(BF)
+        finals.append(copies.push(strip(summed, q), strip(final, q), {"y": at.yf}))
+
+    for q in range(4):
+        terms[:, columns_of(q)] = lax.dot_general(
+            hidden[...],
+            ud[1, 4 * q : 4 * q + 4].reshape(chunk, chunk),
             (((1,), (1,)), ((), ())),
             preferred_element_type=F32,
+        ).astype(BF)
+        relays.append(copies.push(term(at.yo, q), strip(relay, q), {"y": at.yf}))
+        directs.append(copies.push(term(at.yb, q), strip(direct, q), {"y": at.yb}))
+        if q > 0:
+            pass_on(q - 1)
+    pass_on(3)
+    own_rows = pl.ds(pl.multiple_of((1 + shift) * 32, 32), 64)
+    for q in range(4):
+        columns = columns_of(q)
+        copies.got(directs[q], strip(direct, q))
+        partial = (
+            residual[own_rows, columns]
+            + terms[aligned(at.y, 64), columns].astype(F32)
+            + direct[:, columns].astype(F32)
         )
-    out[...] = acc
-
-
-def ring_kernel(part, whole, send, recv, local):
-    at = Place()
-    copies = Copies(send, recv, local)
-    greet([{"y": at.yf}, {"y": at.yb}])
-    halves = (0, 1)
-
-    def piece(y, h):
-        return whole.at[y, pl.ds(32 * h, 32)]
-
-    source = [part.at[pl.ds(32 * h, 32)] for h in halves]
-    ahead = [copies.push(source[h], piece(at.y, h), {"y": at.yf}) for h in halves]
-    behind = [copies.push(source[h], piece(at.y, h), {"y": at.yb}) for h in halves]
-    own = copies.keep(part, whole.at[at.y])
-    fwd = []
-    for h in halves:
-        copies.got(ahead[h], piece(at.yb, h))
-        fwd.append(copies.push(piece(at.yb, h), piece(at.yb, h), {"y": at.yf}))
-    for h in halves:
-        copies.got(behind[h], piece(at.yf, h))
-        copies.got(fwd[h], piece(at.yo, h))
-    own.wait()
-    copies.sent()
-
-
-def sum_kernel(terms, out, relay, direct, summed, final, send, recv):
-    at = Place()
-    copies = Copies(send, recv, None)
-    greet([{"y": at.yf}, {"y": at.yb}])
-    halves = (0, 1)
-
-    def term(y, h):
-        return terms.at[y, pl.ds(32 * h, 32)]
-
-    def half(ref, h):
-        return ref.at[pl.ds(32 * h, 32)]
-
-    relays = [copies.push(term(at.yo, h), half(relay, h), {"y": at.yf}) for h in halves]
-    directs = [copies.push(term(at.yb, h), half(direct, h), {"y": at.yb}) for h in halves]
-    finals = []
-    for h in halves:
-        copies.got(relays[h], half(relay, h))
-        rows = pl.ds(32 * h, 32)
-        summed[rows, :] = (terms[at.yf, rows, :].astype(F32) + relay[rows, :].astype(F32)).astype(
-            BF
-        )
-        finals.append(copies.push(half(summed, h), half(final, h), {"y": at.yf}))
-    for h in halves:
-        rows = pl.ds(32 * h, 32)
-        copies.got(directs[h], half(direct, h))
-        partial = terms[at.y, rows, :].astype(F32) + direct[rows, :].astype(F32)
-        copies.got(finals[h], half(final, h))
-        out[rows, :] = partial + final[rows, :].astype(F32)
+        copies.got(finals[q], strip(final, q))
+        out[:, columns] = (partial + final[:, columns].astype(F32)).astype(BF)
     copies.sent()
 
 
@@ -474,25 +568,12 @@
 
 def shape(*dims, dtype=BF):
     return jax.ShapeDtypeStruct(dims, dtype)
-
-
-def grid_conv(window, conv_weight):
-    padded = jnp.pad(window, ((0, 0), (1, 1), (0, 0)))
-    kernel = conv_weight.astype(F32)
-    result = jnp.zeros((2, 32, window.shape[2]), F32)
-    for vertical in range(3):
-        for lateral in range(3):
-            part = padded[vertical : vertical + 2, lateral : lateral + 32, :].astype(F32)
-            result = result + part * kernel[vertical, lateral]
-    return result.astype(BF)
 
 
 def shards(
     tokens, frame_time, qkv_weight, out_weight, norm_gain, conv_weight, up_weight, down_weight
 ):
     width = tokens.shape[3]
-    core, y, zhi = (lax.axis_index(a) for a in ("core", "y", "zhi"))
-    share = 2 * y + zhi
     tok_all, wq_all, wo_part = pl.pallas_call(
         spread_kernel,
         out_shape=(shape(2, 8, 64, width), shape(3, width, HEAD), shape(2, 16, 96, 256)),
@@ -518,61 +599,35 @@
         + scratch(24, 2),
         compiler_params=remote(2, 40),
     )(frame_time, qkv, wo_part)
-    rows, ud_all = pl.pallas_call(
-        rows_kernel,
-        out_shape=(shape(128, 16 * HEAD), shape(2, 2, 16, 2, 96, 384)),
-        in_specs=[ANY] * 3,
-        out_specs=(ANY,) * 2,
-        scratch_shapes=scratch(64, 3),
-        compiler_params=remote(3),
-    )(attn.reshape(2, 512, HEAD), up_weight, down_weight.T)
-    projected = pl.pallas_call(
-        project_kernel,
-        grid=(12,),
-        out_shape=shape(128, width, dtype=F32),
-        in_specs=[
-            pl.BlockSpec((128, 16 * HEAD), lambda n: (0, 0)),
-            pl.BlockSpec((8, 256, 256), lambda n: (0, n, 0)),
-        ],
-        out_specs=pl.BlockSpec((128, 256), lambda n: (0, n)),
-    )(rows, wo_all.reshape(8, width, 256))
-    first = jnp.clip(2 * share - 1, 0, 12)
-    frame = lax.dynamic_index_in_dim(tok_all, core, 0, keepdims=False).reshape(16, 32, width)
-    near = lax.dynamic_slice_in_dim(frame, first, 4, 0)
-    residual = near.astype(F32) + projected.reshape(4, 32, width)
-    mean_square = jnp.mean(residual * residual, axis=-1, keepdims=True)
-    normed = (residual * lax.rsqrt(mean_square + 1e-06) * norm_gain.astype(F32)).astype(BF)
-    shift = 2 * share - 1 - first
-    window = lax.dynamic_slice_in_dim(
-        jnp.pad(normed, ((1, 1), (0, 0), (0, 0))), 1 + shift, 4, 0
-    )
-    own_residual = lax.dynamic_slice_in_dim(residual, 1 + shift, 2, 0)
-    conved = grid_conv(window, conv_weight).reshape(64, width)
-    gathered = pl.pallas_call(
-        ring_kernel,
-        out_shape=shape(4, 64, width),
-        in_specs=[ANY],
-        out_specs=ANY,
-        scratch_shapes=scratch(8, 1),
-        compiler_params=remote(4),
-    )(conved).reshape(256, width)
-    up_all = ud_all[0].reshape(2, width, 384)
-    down_all = ud_all[1].reshape(2, width, 384)
-    lowered = jnp.zeros((256, width), F32)
-    for z in range(2):
-        hidden = jax.nn.gelu(jnp.dot(gathered, up_all[z], preferred_element_type=F32)).astype(BF)
-        lowered = lowered + lax.dot_general(
-            hidden, down_all[z], (((1,), (1,)), ((), ())), preferred_element_type=F32
-        )
-    summed = pl.pallas_call(
-        sum_kernel,
-        out_shape=shape(64, width, dtype=F32),
-        in_specs=[VMEM],
+    result = pl.pallas_call(
+        layer_kernel,
+        out_shape=shape(64, width),
+        in_specs=[ANY] * 5 + [VMEM] * 2,
         out_specs=VMEM,
-        scratch_shapes=[pltpu.VMEM((64, width), BF)] * 4 + scratch(8, 1)[:2],
-        compiler_params=remote(5),
-    )(lowered.astype(BF).reshape(4, 64, width))
-    return (own_residual + summed.reshape(2, 32, width)).astype(BF)[None]
+        scratch_shapes=[
+            pltpu.VMEM((8, width, 256), BF),
+            pltpu.VMEM((128, 16 * HEAD), BF),
+            pltpu.VMEM((128, width), BF),
+            pltpu.VMEM((128, width), F32),
+            pltpu.VMEM((6, 32, width), F32),
+            pltpu.VMEM((256, width), BF),
+            pltpu.VMEM((2, 16, 2, 96, 768), BF),
+            pltpu.VMEM((256, 768), BF),
+            pltpu.VMEM((256, width), BF),
+        ]
+        + [pltpu.VMEM((64, width), BF)] * 4
+        + scratch(80, 5),
+        compiler_params=remote(3, 56),
+    )(
+        attn.reshape(2, 512, HEAD),
+        up_weight,
+        down_weight.T,
+        wo_all.reshape(8, width, 256),
+        tok_all.reshape(2, 512, width),
+        norm_gain.reshape(1, width),
+        conv_weight,
+    )
+    return result.reshape(1, 2, 32, width)
 
 
 def solution(mesh):

time: 320 us -> 273 us (0.85)
  Pallas kernels: 286 us -> 260 us
  matrix products: 14.6 us -> 3.4 us
  local copies, waits for them, and re-layouts: 13.6 us -> 5.79 us
  other arithmetic: 4.48 us -> 0 us
    pallas_call x4 -> x1, Pallas kernels: 122 us -> 98.9 us  [shards(): pl.pallas_call(layer_kernel, out_shape=shape(64, width), in_specs=[ANY] *...]
    dot_general x2 -> x0, matrix products: 11.2 us -> none  [shards(): lax.dot_general(hidden, down_all[z], (((1,), (1,)), ((), ())), preferred_...]
    slice x2 -> x0, local copies, waits for them, and re-layouts: 4.86 us -> none  [the longest x1 3.81 us: shards(): up_all[z]]
    unnamed x22 -> x15, local copies, waits for them, and re-layouts: 8.31 us -> 5.18 us
where the time goes in v2:
time: 273 us; the launch traced here: 269 us
  Pallas kernels  260 us (95%)
  local copies, waits for them, and re-layouts  5.79 us (2%)
  matrix products  3.4 us (1%)
    pallas_call x1, Pallas kernels, shards(): pl.pallas_call(layer_kernel, out_shape=shape(64, width), in_specs=[ANY] *...  98.9 us
    pallas_call x1, Pallas kernels, shards(): pl.pallas_call(attend_kernel, out_shape=(shape(1024, HEAD), shape(8, 16,...  96.2 us
    pallas_call x1, Pallas kernels, shards(): pl.pallas_call(spread_kernel, out_shape=(shape(2, 8, 64, width), shape(3,...  64.5 us

profile of v2, /device:TPU:1, one launch (start us, length us, event | category | flops | bytes accessed | tf_op | source)
XLA Modules:
  0.0 269.1 jit_solution(9770996930364657228)
XLA Ops:
  0.0 0.0 copy-start.1
  0.0 1.0 copy-done.1
  1.0 0.0 copy-start.3
  1.0 0.9 copy-done.3
  1.9 0.0 copy-start.4
  1.9 0.8 copy-done.4
  2.7 64.5 %shard_map.82 = (bf16[2,8,64,3072]{3,2,1,0:T(8,128)(2,1)S(1)}, bf16[3,3072,128]{2,1,0:T(8,128)(2,1)S(1)}, bf16[2,16,96,256]{3,2,1,0:T(8,128)(2,1)S(1)}) custom-call(bf16[64,3072]{1,0:T(8,128)(2,1)S(1)} %bitcast.16, bf16[3,96,256]{2,1,0:T(8,128)(2,1)S(1)} %copy-done.3, bf16[96,256]{1,0:T(8,128)(2,1)S(1)} %bitcast.18), custom_call_target="tpu_custom_call" | custom-call | tf_op jit(solution)/shard_map/pallas_call | solution.py:577
  67.2 0.0 copy-start
  67.2 0.0 copy-start.5
  67.2 3.4 %fusion.qkv = bf16[3,1024,128]{2,1,0:T(8,128)(2,1)S(1)} fusion(bf16[1024,3072,1]{1,0,2:T(8,128)(2,1)S(1)} %bitcast.14, bf16[3,3072,128]{2,1,0:T(8,128)(2,1)S(1)} %get-tuple-element.10), kind=kOutput, calls=%fused_computation.1 | convolution fusion | flops 2416312320 | bytes 9437184 | tf_op jit(solution)/shard_map/td,idh->ith/dot_general | solution.py:585
  70.6 0.0 copy-done
  70.6 0.0 copy-start.6
  70.6 0.0 copy-done.5
  70.6 96.2 %shard_map.83 = (bf16[1024,128]{1,0:T(8,128)(2,1)S(1)}, bf16[8,16,2,96,256]{4,3,2,1,0:T(8,128)(2,1)}) custom-call(s32[32]{0:T(128)S(1)} %copy-done.5, bf16[3,1024,128]{2,1,0:T(8,128)(2,1)S(1)} %fusion.qkv, bf16[2,16,96,256]{3,2,1,0:T(8,128)(2,1)S(1)} %get-tuple-element.12.wo), custom_call_target="tpu_custom_call" | custom-call | tf_op jit(solution)/shard_map/pallas_call | solution.py:588
  166.9 0.0 copy-start.2
  166.9 0.7 copy-done.2
  167.6 0.0 copy-done.6
  167.6 0.6 reshape.26.gain
  168.2 98.9 %shard_map.84 = bf16[64,3072]{1,0:T(8,128)(2,1)} custom-call(bf16[2,512,128]{2,1,0:T(8,128)(2,1)} %bitcast.17, bf16[96,384]{1,0:T(8,128)(2,1)} %up.1, bf16[96,384]{1,0:T(8,128)(2,1)} %bitcast.21, bf16[8,3072,256]{2,1,0:T(8,128)(2,1)} %bitcast.19, bf16[2,512,3072]{2,1,0:T(8,128)(2,1)} %bitcast.15, bf16[1,3072]{1,0:T(2,128)(2,1)} %reshape.26.gain, ...), custom_call_target="tpu_custom_call" | custom-call | tf_op jit(solution)/shard_map/pallas_call | solution.py:602
  267.1 1.8 copy.14
Async XLA Ops:
  0.0 1.0 copy-start.1
  1.0 0.9 copy-start.3
  1.9 0.8 copy-start.4
  67.2 3.4 %copy-start = (bf16[2,8,64,3072]{3,2,1,0:T(8,128)(2,1)}, bf16[2,8,64,3072]{3,2,1,0:T(8,128)(2,1)S(1)}, u32[]{:S(2)}) copy-start(bf16[2,8,64,3072]{3,2,1,0:T(8,128)(2,1)S(1)} %get-tuple-element.11) | copy-start | bytes 18874372
  67.2 3.4 %copy-start.5 = (s32[32]{0:T(128)S(1)}, s32[32]{0:T(128)}, u32[]{:S(2)}) copy-start(s32[32]{0:T(128)} %times.1) | copy-start | bytes 388
  70.6 97.0 %copy-start.6 = (bf16[3072]{0:T(1024)(128)(2,1)S(1)}, bf16[3072]{0:T(1024)(128)(2,1)}, u32[]{:S(2)}) copy-start(bf16[3072]{0:T(1024)(128)(2,1)} %param.12) | copy-start | bytes 18436
  166.9 0.7 copy-start.2

commit v3 on v2

v3 whole, which is shorter than its diff:
```python
import math

import jax
import jax.numpy as jnp
from jax import lax
from jax.experimental import pallas as pl
from jax.experimental.pallas import tpu as pltpu
from jax.sharding import Mesh
from jax.sharding import PartitionSpec as P

HEAD = 128
MESH = pl.DeviceIdType.MESH
BF = jnp.bfloat16
F32 = jnp.float32
AXES = ("zlo", "x", "core", "y", "zhi")
ANY = pl.BlockSpec(memory_space=pl.ANY)
VMEM = pl.BlockSpec(memory_space=pltpu.VMEM)
SMEM = pl.BlockSpec(memory_space=pltpu.SMEM)
SCALE2 = math.log2(math.e) / math.sqrt(HEAD)


def aligned(index, size):
    return pl.ds(pl.multiple_of(index * size, size), size)


class Place:
    def __init__(self):
        self.zlo, self.x, self.core, self.y, self.zhi = (lax.axis_index(a) for a in AXES)
        turn = 1 - 2 * self.core
        self.chip = self.zlo * 4 + self.x
        self.share = 2 * self.y + self.zhi
        self.xf, self.xb, self.xo = (lax.rem(self.x + 4 + k, 4) for k in (turn, -turn, 2))
        self.yf, self.yb, self.yo = (lax.rem(self.y + 4 + k, 4) for k in (turn, -turn, 2))
        self.partner = {"core": 1 - self.core}
        self.side = self.x // 2
        self.xs = self.x + 1 - 2 * lax.rem(self.x, 2)
        self.xp = 3 - self.x
        self.zq = self.zlo + 1 - 2 * lax.rem(self.zlo, 2)
        self.far = {"zhi": 1 - self.zhi}


class Copies:
    def __init__(self, send, recv, local):
        self.send, self.recv, self.local = send, recv, local
        self.pushed, self.kept, self.count = {}, 0, 0

    def reserve(self):
        self.count += 1
        return self.count - 1

    def push(self, src, dst, device, lands=None, when=None):
        index = self.reserve()
        arrives = self.recv.at[index if lands is None else lands]
        copy = pltpu.make_async_remote_copy(
            src, dst, self.send.at[index], arrives, device_id=device, device_id_type=MESH
        )
        if when is None:
            copy.start()
        else:
            pl.when(when)(copy.start)
        self.pushed[index] = (copy, when)
        return index

    def hand(self, src, dst, device, here, lands):
        copy = pltpu.make_async_copy(src, dst, self.recv.at[lands])
        pl.when(here)(copy.start)
        self.push(src, dst, device, lands, jnp.logical_not(here))

    def got(self, index, region):
        pltpu.make_async_copy(region, region, self.recv.at[index]).wait()

    def keep(self, src, dst):
        copy = pltpu.make_async_copy(src, dst, self.local.at[self.kept])
        copy.start()
        self.kept += 1
        return copy

    def left(self, index):
        copy, when = self.pushed.pop(index)
        if when is None:
            copy.wait_send()
        else:
            pl.when(when)(copy.wait_send)

    def sent(self):
        for index in list(self.pushed):
            self.left(index)


def greet(devices):
    barrier = pltpu.get_barrier_semaphore()
    for device in devices:
        pl.semaphore_signal(barrier, inc=1, device_id=device, device_id_type=MESH)
    pl.semaphore_wait(barrier, len(devices))


def x_start(copies, at, region, z):
    mine = region(z * 4 + at.x)
    return (
        copies.push(mine, mine, {"x": at.xf}),
        copies.push(mine, mine, {"x": at.xb}),
    )


def x_forward(copies, at, region, z, started):
    block = region(z * 4 + at.xb)
    copies.got(started[0], block)
    return copies.push(block, block, {"x": at.xf})


def x_rest(copies, at, region, z, started, forwarded):
    copies.got(started[1], region(z * 4 + at.xf))
    copies.got(forwarded, region(z * 4 + at.xo))


def scratch(pushes, locals_):
    return [
        pltpu.SemaphoreType.DMA((pushes,)),
        pltpu.SemaphoreType.DMA((pushes,)),
        pltpu.SemaphoreType.DMA((locals_,)),
    ]


def layer_kernel(
    times,
    tokens,
    wq,
    wo,
    up,
    down,
    gain,
    conv,
    out,
    tok,
    wq_here,
    stage,
    queries,
    kv,
    top,
    total,
    mixed,
    attn,
    wo_here,
    rows,
    residual,
    window,
    gathered,
    ud,
    hidden,
    terms,
    relay,
    direct,
    summed,
    final,
    send,
    recv,
    local,
):
    at = Place()
    copies = Copies(send, recv, local)
    width = out.shape[1]
    deep = at.zhi * 4 + at.zlo
    z_steps = (1, 7, 2, 6, 3, 5, 4)
    deep_to = [lax.rem(deep + k, 8) for k in z_steps]
    order = [deep] + [lax.rem(deep + 8 - k, 8) for k in z_steps]
    zs = [lax.rem(at.zlo + k, 4) for k in (1, 3, 2)]
    zfrom = [at.zlo] + [lax.rem(at.zlo + 4 - k, 4) for k in (1, 3, 2)]
    peers = [(c, z, y) for z in (1, 0) for y in range(4) for c in (0, 1) if (c, z, y) != (0, 0, 0)]
    halves = (0, 1)

    def peer(c, z, y, sign):
        return (
            lax.rem(at.core + c, 2),
            lax.rem(at.zhi + z, 2),
            lax.rem(at.y + 4 + sign * y, 4),
        )

    def named(place):
        return {"core": place[0], "zhi": place[1], "y": place[2]}

    def depth(z):
        return {"zhi": z // 4, "zlo": lax.rem(z, 4)}

    greet(
        [named(peer(*p, 1)) for p in peers]
        + [{"x": at.xp, **named(peer(*p, 1))} for p in peers + [(0, 0, 0)]]
        + [{"x": at.xs}]
        + [depth(z) for z in deep_to[:-1]]
    )


    def piece(share, half):
        return tok.at[at.core, pl.ds(pl.multiple_of(share * 64 + half * 32, 32), 32)]

    def share_block(core, share):
        return tok.at[core, aligned(share, 64)]

    def wq_block(chip):
        return wq_here.at[aligned(chip, 192)]

    def wo_block(chip):
        return wo_here.at[pl.ds(2 * at.y, 2), chip, at.core]

    def wo_plane(y, core):
        return wo_here.at[pl.ds(2 * y, 2), :, core]

    def kv_block(chip):
        return kv.at[chip]

    source = [tokens.at[pl.ds(32 * h, 32)] for h in halves]

    def wq_piece(core, i):
        return wq_here.at[aligned(2 * at.chip + core, 96), pl.ds(HEAD * i, HEAD)]

    far = []
    w_pair = [
        copies.push(
            wq.at[i, :, aligned(1 - at.core, HEAD)], wq_piece(at.core, i), at.partner
        )
        for i in range(3)
    ]
    w_own = [
        copies.keep(wq.at[i, :, aligned(at.core, HEAD)], wq_piece(at.core, i)) for i in range(3)
    ]
    own_f = [copies.push(source[h], piece(at.share, h), {"y": at.yf}) for h in halves]
    own_b = [copies.push(source[h], piece(at.share, h), {"y": at.yb}) for h in halves]
    t_own = copies.keep(tokens, share_block(at.core, at.share))
    o_own = copies.keep(wo, wo_here.at[at.share, at.chip, at.core])
    own_ud = [
        copies.keep(ref, ud.at[i, at.chip, at.core, :, aligned(at.zhi, 384)])
        for i, ref in enumerate((up, down))
    ]
    shared = []

    def share_out(share):
        block = share_block(at.core, share)
        shared.append((copies.push(block, block, at.partner), share))

    for i in range(3):
        w_own[i].wait()
        copies.got(w_pair[i], wq_piece(1 - at.core, i))
    w_z = [copies.push(wq_block(at.chip), wq_block(at.chip), {"zlo": z}) for z in zs]
    w_x = [x_start(copies, at, wq_block, at.zlo)]
    far.append(copies.push(source[0], piece(at.share, 0), at.far))
    far.append(copies.push(source[1], piece(at.share, 1), at.far))
    o_far = copies.push(wo, wo_here.at[at.share, at.chip, at.core], at.far)
    t_own.wait()
    share_out(at.share)
    far_share = 2 * at.y + 1 - at.zhi
    near_ring = [2 * y + at.zhi for y in (at.yb, at.yf, at.yo)]
    far_ring = [2 * y + 1 - at.zhi for y in (at.yb, at.yf, at.yo)]
    fwd, far_f, far_b = [], [], []

    def pass_tokens(index, share, half):
        block = piece(share, half)
        copies.got(index, block)
        return copies.push(block, block, {"y": at.yf})

    def spread_far(h):
        block = piece(far_share, h)
        copies.got(far[h], block)
        far_f.append(copies.push(block, block, {"y": at.yf}))
        far_b.append(copies.push(block, block, {"y": at.yb}))

    w_f = []

    def w_open(k):
        copies.got(w_z[k - 1], wq_block(zfrom[k] * 4 + at.x))
        w_x.append(x_start(copies, at, wq_block, zfrom[k]))

    def w_forward(k):
        w_f.append(x_forward(copies, at, wq_block, zfrom[k], w_x[k]))

    fwd.append(pass_tokens(own_f[0], near_ring[0], 0))
    w_forward(0)
    w_open(1)
    fwd.append(pass_tokens(own_f[1], near_ring[0], 1))
    share_out(near_ring[0])
    w_forward(1)
    w_open(2)
    for h in halves:
        copies.got(own_b[h], piece(near_ring[1], h))
    share_out(near_ring[1])
    w_open(3)
    w_forward(2)
    spread_far(0)
    for h in halves:
        copies.got(fwd[h], piece(near_ring[2], h))
    share_out(near_ring[2])
    w_forward(3)
    spread_far(1)
    share_out(far_share)
    o_own.wait()
    copies.got(o_far, wo_here.at[far_share, at.chip, at.core])
    o_z = [copies.push(wo_block(at.chip), wo_block(at.chip), {"zlo": z}) for z in zs]
    o_x = [x_start(copies, at, wo_block, at.zlo)]
    fwd = []
    for h in halves:
        fwd.append(pass_tokens(far_f[h], far_ring[0], h))
    share_out(far_ring[0])
    for h in halves:
        copies.got(far_b[h], piece(far_ring[1], h))
    share_out(far_ring[1])
    o_f = [x_forward(copies, at, wo_block, at.zlo, o_x[0])]
    for h in halves:
        copies.got(fwd[h], piece(far_ring[2], h))
    share_out(far_ring[2])
    for k in range(4):
        x_rest(copies, at, wq_block, zfrom[k], w_x[k], w_f[k])
    for index, share in shared:
        copies.got(index, share_block(1 - at.core, share))


    native = at.core == at.side
    across = {"x": at.xp, "core": 1 - at.core}
    px = at.core * at.side + (1 - at.core) * (1 - at.side)
    px = px * at.x + (1 - px) * at.xp
    pxs = px + 1 - 2 * lax.rem(px, 2)
    held = at.zlo * 4 + px
    inner = jnp.logical_or(at.zlo == 1, at.zlo == 2)
    zi = 3 - at.zlo
    zsrc = [at.zlo, at.zq, 2 - at.zlo // 2, 3 - 3 * (at.zlo // 2)]
    handed = [copies.reserve() for _ in range(3)]
    for t in range(2):
        part = pl.ds(512 * t, 512)
        both = jnp.dot(tok[t], wq_here[:, HEAD:], preferred_element_type=F32).astype(BF)
        stage[1, part, :] = both[:, :HEAD]
        stage[2, part, :] = both[:, HEAD:]
        copies.hand(
            stage.at[pl.ds(1, 2), part], kv.at[at.chip, :, part], across, native, handed[t]
        )
    for t in range(2):
        stage[0, pl.ds(512 * t, 512), :] = jnp.dot(
            tok[t], wq_here[:, :HEAD], preferred_element_type=F32
        ).astype(BF)
    copies.hand(stage.at[0], queries, across, native, handed[2])
    top[...] = jnp.full_like(top, -1e30)
    total[...] = jnp.zeros_like(total)
    mixed[...] = jnp.zeros_like(mixed)
    for t in range(2):
        copies.got(handed[t], kv.at[held, :, pl.ds(512 * t, 512)])

    def attend(chip):
        for t in range(2):
            part_rows = slice(512 * t, 512 * t + 512)
            own_time = times[2 * held + t]
            scores = lax.dot_general(
                queries[part_rows, :],
                kv[chip, 0],
                (((1,), (1,)), ((), ())),
                preferred_element_type=F32,
            )
            seen = [times[2 * chip + j] <= own_time for j in (0, 1)]
            parts = [scores[:, :512], scores[:, 512:]]
            old = top[part_rows, :1]
            new = old
            for part, see in zip(parts, seen):
                new = jnp.maximum(
                    new, jnp.where(see, jnp.max(part, axis=1, keepdims=True), -1e30)
                )
            decay = jnp.exp2((old - new) * SCALE2)
            weights = [
                jnp.exp2((part - jnp.where(see, new, 1e30)) * SCALE2)
                for part, see in zip(parts, seen)
            ]
            lanes = total[part_rows, :] * decay
            for part in weights:
                for j in range(4):
                    lanes = lanes + part[:, 128 * j : 128 * j + 128]
            total[part_rows, :] = lanes
            top[part_rows, :] = jnp.broadcast_to(new, (512, 128))
            both = jnp.concatenate([part.astype(BF) for part in weights], axis=1)
            mixed[part_rows, :] = mixed[part_rows, :] * decay + jnp.dot(
                both, kv[chip, 1], preferred_element_type=F32
            )

    lands = [copies.reserve() for _ in range(3)]
    beside, columns_over, beside_over = [], [], []

    def column(k, x):
        return kv_block(zsrc[k] * 4 + x)

    def kv_open(k):
        block = column(k, px)
        if k > 0:
            copies.got(lands[k - 1], block)
        beside.append(copies.push(block, block, {"x": at.xs}))
        if k == 0:
            copies.push(block, block, {"zlo": at.zq}, lands[0])
            copies.push(block, block, {"zlo": zi}, lands[1], inner)
        if k == 1:
            copies.push(block, block, {"zlo": zi}, lands[2], inner)
        if k > 1:
            copies.push(block, block, {"zlo": at.zq}, lands[k - 1], inner)
        columns_over.append(copies.push(block, block, at.partner))

    def kv_beside(k):
        block = column(k, pxs)
        copies.got(beside[k], block)
        beside_over.append(copies.push(block, block, at.partner))

    def attend_column(k):
        attend(zsrc[k] * 4 + px)

    def attend_beside(k):
        attend(zsrc[k] * 4 + pxs)

    def attend_column_over(k):
        copies.got(columns_over[k], column(k, 3 - px))
        attend(zsrc[k] * 4 + 3 - px)

    def attend_beside_over(k):
        copies.got(beside_over[k], column(k, 3 - pxs))
        attend(zsrc[k] * 4 + 3 - pxs)

    def ud_block(z, x):
        return ud.at[:, lax.rem(z, 4) * 4 + x, at.core, :, aligned(z // 4, 384)]

    def ud_lump(z, core):
        return ud.at[:, aligned(lax.rem(z, 4), 4), core, :, aligned(z // 4, 384)]

    def x_push(z):
        block = ud_block(z, at.x)
        return (copies.push(block, block, {"x": at.xf}), copies.push(block, block, {"x": at.xb}))

    kv_open(0)
    for k in (1, 2, 3):
        copies.got(o_z[k - 1], wo_block(zfrom[k] * 4 + at.x))
        o_x.append(x_start(copies, at, wo_block, zfrom[k]))
    copies.got(handed[2], queries)
    attend_column(0)
    attend_column_over(0)
    for k in (1, 2, 3):
        o_f.append(x_forward(copies, at, wo_block, zfrom[k], o_x[k]))
    kv_open(1)
    kv_beside(0)
    attend_beside(0)
    for k in range(4):
        x_rest(copies, at, wo_block, zfrom[k], o_x[k], o_f[k])
    plane = wo_plane(at.y, at.core)
    wo_f = copies.push(plane, plane, {"y": at.yf})
    wo_b = copies.push(plane, plane, {"y": at.yb})
    wo_p = [copies.push(plane, plane, at.partner)]
    attend_column(1)
    attend_column_over(1)
    attend_beside_over(0)
    kv_open(2)
    kv_beside(1)
    attend_beside(1)
    attend_column(2)
    attend_column_over(2)
    attend_beside_over(1)
    kv_open(3)
    for copy in own_ud:
        copy.wait()
    block = ud_block(deep, at.x)
    along_z = [copies.push(block, block, depth(z)) for z in deep_to]
    kv_beside(2)
    attend_beside(2)
    attend_column(3)
    attend_column_over(3)
    attend_beside_over(2)
    kv_beside(3)
    attend_beside(3)
    attend_beside_over(3)
    plane = wo_plane(at.yb, at.core)
    copies.got(wo_f, plane)
    wo_fwd = copies.push(plane, plane, {"y": at.yf})
    wo_p.append(copies.push(plane, plane, at.partner))
    plane = wo_plane(at.yf, at.core)
    copies.got(wo_b, plane)
    wo_p.append(copies.push(plane, plane, at.partner))
    for t in range(2):
        part_rows = slice(512 * t, 512 * t + 512)
        attn[t] = (
            mixed[part_rows, :] / jnp.sum(total[part_rows, :], axis=1, keepdims=True)
        ).astype(BF)


    def head_rows(head):
        return rows.at[:, aligned(head, HEAD)]

    def first_row(share):
        return jnp.clip(2 * share - 1, 0, 12)

    def needed(place):
        core, zhi, y = place
        return attn.at[core, pl.ds(pl.multiple_of(first_row(2 * y + zhi) * 32, 32), 128)]

    head = 2 * at.share + at.side
    first = first_row(at.share)
    role = at.core + at.side - 2 * at.core * at.side
    places = [(z, y) for z in (1, 0) for y in range(4)]
    arrivals = []
    for z, y in places:
        base = copies.reserve()
        copies.reserve()
        arrivals.append(base)
        for c in (0, 1):
            _, zhi, y_to = peer(0, z, y, 1)
            goal = (lax.rem(at.core + c, 2), zhi, y_to)
            device = {"x": px, **named(goal)}
            if (c, z, y) == (0, 0, 0):
                copies.hand(needed(goal), head_rows(head), device, native, base + role)
            else:
                copies.push(needed(goal), head_rows(head), device, base + role)
    opened, forwarded, lumps = [x_push(deep)], [], []

    def open_group(k):
        copies.got(along_z[k - 1], ud_block(order[k], at.x))
        opened.append(x_push(order[k]))

    def forward_group(k):
        block = ud_block(order[k], at.xb)
        copies.got(opened[k][0], block)
        forwarded.append(copies.push(block, block, {"x": at.xf}))

    def close_group(k):
        copies.got(opened[k][1], ud_block(order[k], at.xf))
        copies.got(forwarded[k], ud_block(order[k], at.xo))
        lump = ud_lump(order[k], at.core)
        lumps.append(copies.push(lump, lump, at.partner))

    shift = 2 * at.share - 1 - first
    for r in (1, 4):
        window[r] = jnp.zeros(window.shape[1:], F32)
    for k in (1, 2, 3):
        open_group(k)
    forward_group(0)
    plane = wo_plane(at.yo, at.core)
    copies.got(wo_fwd, plane)
    wo_p.append(copies.push(plane, plane, at.partner))
    for base, (z, y) in zip(arrivals, places):
        _, zhi, y_from = peer(0, z, y, -1)
        whose = 2 * (2 * y_from + zhi)
        copies.got(base, head_rows(whose + at.side))
        copies.got(base + 1, head_rows(whose + 1 - at.side))
    for index, y in zip(wo_p, (at.y, at.yb, at.yf, at.yo)):
        copies.got(index, wo_plane(y, 1 - at.core))
    for k in (4, 5):
        open_group(k)
    forward_group(1)
    near_rows = pl.ds(pl.multiple_of(first * 32, 32), 128)

    def project(n, carry):
        columns = aligned(n, 768)
        acc = tok[at.core, near_rows, columns].astype(F32)
        for s in range(8):
            acc = acc + lax.dot_general(
                rows[:, 256 * s : 256 * s + 256],
                wo_here[s, pl.ds(4 * n, 4)].reshape(768, 256),
                (((1,), (1,)), ((), ())),
                preferred_element_type=F32,
            )
        residual[:, columns] = acc
        return carry

    lax.fori_loop(0, 4, project, 0)
    for k in (6, 7):
        open_group(k)
    forward_group(2)
    close_group(0)
    forward_group(3)
    for r in range(4):
        row = residual[32 * r : 32 * r + 32, :]
        mean_square = jnp.mean(row * row, axis=1, keepdims=True)
        normed = row * lax.rsqrt(mean_square + 1e-06) * gain[...].astype(F32)
        window[1 + r - shift] = normed.astype(BF).astype(F32)
    close_group(1)
    line = lax.broadcasted_iota(jnp.int32, (32, 512), 0)

    def convolve(j):
        def tile(n, carry):
            columns = aligned(n, 512)
            sums = [jnp.zeros((32, 512), F32)] * 3
            for a in range(3):
                taps = conv[a, :, columns].astype(F32)
                values = window[1 + j + a, :, columns]
                for b in range(3):
                    sums[b] = sums[b] + values * taps[b : b + 1, :]
            before = jnp.where(line == 0, 0.0, pltpu.roll(sums[0], 1, 0))
            after = jnp.where(line == 31, 0.0, pltpu.roll(sums[2], 31, 0))
            gathered[aligned(2 * at.y + j, 32), columns] = (before + sums[1] + after).astype(BF)
            return carry

        lax.fori_loop(0, width // 512, tile, 0)

    def token_piece(y, h):
        return gathered.at[aligned(2 * y + h, 32)]

    ahead, behind = [], []
    for h in (0, 1):
        convolve(h)
        piece = token_piece(at.y, h)
        ahead.append(copies.push(piece, piece, {"y": at.yf}))
        behind.append(copies.push(piece, piece, {"y": at.yb}))
    forward_group(4)
    close_group(2)
    token_fwd = []
    for h in (0, 1):
        piece = token_piece(at.yb, h)
        copies.got(ahead[h], piece)
        token_fwd.append(copies.push(piece, piece, {"y": at.yf}))
    close_group(3)
    for k in (5, 6, 7):
        forward_group(k)
        close_group(k - 1)
    close_group(7)
    for h in (0, 1):
        copies.got(behind[h], token_piece(at.yf, h))
        copies.got(token_fwd[h], token_piece(at.yo, h))
    for index, z in zip(lumps, order):
        copies.got(index, ud_lump(z, 1 - at.core))

    for n in range(3):
        columns = slice(256 * n, 256 * n + 256)
        value = jnp.dot(
            gathered[...],
            ud[0, :, :, :, columns].reshape(width, 256),
            preferred_element_type=F32,
        )
        hidden[:, columns] = jax.nn.gelu(value).astype(BF)

    chunk = width // 4

    def columns_of(q):
        return slice(chunk * q, chunk * q + chunk)

    def term(y, q):
        return terms.at[aligned(y, 64), pl.ds(chunk * q, chunk)]

    def strip(ref, q):
        return ref.at[:, pl.ds(chunk * q, chunk)]

    relays, directs, finals = [], [], []

    def pass_on(q):
        copies.got(relays[q], strip(relay, q))
        columns = columns_of(q)
        summed[:, columns] = (
            terms[aligned(at.yf, 64), columns].astype(F32) + relay[:, columns].astype(F32)
        ).astype(BF)
        finals.append(copies.push(strip(summed, q), strip(final, q), {"y": at.yf}))

    for q in range(4):
        terms[:, columns_of(q)] = lax.dot_general(
            hidden[...],
            ud[1, 4 * q : 4 * q + 4].reshape(chunk, chunk),
            (((1,), (1,)), ((), ())),
            preferred_element_type=F32,
        ).astype(BF)
        relays.append(copies.push(term(at.yo, q), strip(relay, q), {"y": at.yf}))
        directs.append(copies.push(term(at.yb, q), strip(direct, q), {"y": at.yb}))
        if q > 0:
            pass_on(q - 1)
    pass_on(3)
    own_rows = pl.ds(pl.multiple_of((1 + shift) * 32, 32), 64)
    for q in range(4):
        columns = columns_of(q)
        copies.got(directs[q], strip(direct, q))
        partial = (
            residual[own_rows, columns]
            + terms[aligned(at.y, 64), columns].astype(F32)
            + direct[:, columns].astype(F32)
        )
        copies.got(finals[q], strip(final, q))
        out[:, columns] = (partial + final[:, columns].astype(F32)).astype(BF)
    copies.sent()


def remote(collective_id, megabytes=32):
    return pltpu.CompilerParams(
        collective_id=collective_id, has_side_effects=True, vmem_limit_bytes=megabytes << 20
    )


def shape(*dims, dtype=BF):
    return jax.ShapeDtypeStruct(dims, dtype)


def shards(
    tokens, frame_time, qkv_weight, out_weight, norm_gain, conv_weight, up_weight, down_weight
):
    width = tokens.shape[3]
    result = pl.pallas_call(
        layer_kernel,
        out_shape=shape(64, width),
        in_specs=[SMEM] + [ANY] * 5 + [VMEM] * 2,
        out_specs=VMEM,
        scratch_shapes=[
            pltpu.VMEM((2, 512, width), BF),
            pltpu.VMEM((width, 3 * HEAD), BF),
            pltpu.VMEM((3, 1024, HEAD), BF),
            pltpu.VMEM((1024, HEAD), BF),
            pltpu.VMEM((16, 2, 1024, HEAD), BF),
            pltpu.VMEM((1024, HEAD), F32),
            pltpu.VMEM((1024, HEAD), F32),
            pltpu.VMEM((1024, HEAD), F32),
            pltpu.VMEM((2, 512, HEAD), BF),
            pltpu.VMEM((8, 16, 2, 96, 256), BF),
            pltpu.VMEM((128, 16 * HEAD), BF),
            pltpu.VMEM((128, width), F32),
            pltpu.VMEM((6, 32, width), F32),
            pltpu.VMEM((256, width), BF),
            pltpu.VMEM((2, 16, 2, 96, 768), BF),
            pltpu.VMEM((256, 768), BF),
            pltpu.VMEM((256, width), BF),
        ]
        + [pltpu.VMEM((64, width), BF)] * 4
        + scratch(224, 8),
        compiler_params=remote(1, 60),
    )(
        frame_time,
        tokens.reshape(64, width),
        qkv_weight,
        out_weight.T,
        up_weight,
        down_weight.T,
        norm_gain.reshape(1, width),
        conv_weight,
    )
    return result.reshape(1, 2, 32, width)


def solution(mesh):
    fine = Mesh(mesh.devices.reshape(4, 4, 2, 4, 2), AXES)
    frame, fsdp = ("zlo", "x", "core"), ("y", "zhi")
    placed = (
        P(frame, fsdp, None, None),
        P(),
        P(None, frame, fsdp),
        P(fsdp, frame),
        P(),
        P(),
        P(frame, fsdp),
        P(fsdp, frame),
    )
    return jax.shard_map(
        shards,
        mesh=fine,
        in_specs=placed,
        out_specs=P(frame, fsdp, None, None),
        check_vma=False,
    )
```

time: 273 us -> 229 us (0.84)
  Pallas kernels: 260 us -> 222 us
  matrix products: 3.4 us -> 0 us
    pallas_call x3 -> x1, Pallas kernels: 260 us -> 222 us  [shards(): pl.pallas_call(layer_kernel, out_shape=shape(64, width), in_specs=[SMEM]...]
    unnamed x15 -> x1, local copies, waits for them, and re-layouts: 5.18 us -> 1.77 us
    dot_general x1 -> x0, matrix products: 3.4 us -> none  [shards(): jnp.einsum('td,idh->ith', tok_all.reshape(1024, width), wq_all, preferred...]
where the time goes in v3:
time: 229 us; the launch traced here: 226 us
  Pallas kernels  222 us (97%)
  local copies, waits for them, and re-layouts  3.07 us (1%)
    pallas_call x1, Pallas kernels, shards(): pl.pallas_call(layer_kernel, out_shape=shape(64, width), in_specs=[SMEM]...  222 us

profile of v3, /device:TPU:1, one launch (start us, length us, event | category | flops | bytes accessed | tf_op | source)
XLA Modules:
  0.0 225.8 jit_solution(6387810289684300838)
XLA Ops:
  0.0 1.3 reshape.10.gain
  1.3 222.5 %shard_map.82 = bf16[64,3072]{1,0:T(8,128)(2,1)} custom-call(s32[32]{0:T(128)} %times.1, bf16[64,3072]{1,0:T(8,128)(2,1)} %bitcast.5, bf16[3,96,256]{2,1,0:T(8,128)(2,1)} %wq.1, bf16[96,256]{1,0:T(8,128)(2,1)} %bitcast.7, bf16[96,384]{1,0:T(8,128)(2,1)} %up.1, bf16[96,384]{1,0:T(8,128)(2,1)} %bitcast.6, bf16[1,3072]{1,0:T(2,128)(2,1)} %reshape.10.gain, ...), custom_call_target="tpu_custom_call" | custom-call | tf_op jit(solution)/shard_map/pallas_call | solution.py:685
  223.8 1.8 copy.10

commit v4 on v3

--- a/solution.py
+++ b/solution.py
@@ -36,6 +36,9 @@
         self.xs = self.x + 1 - 2 * lax.rem(self.x, 2)
         self.xp = 3 - self.x
         self.zq = self.zlo + 1 - 2 * lax.rem(self.zlo, 2)
+        self.zi = 3 - self.zlo
+        self.inner = jnp.logical_or(self.zlo == 1, self.zlo == 2)
+        self.zsrc = [self.zlo, self.zq, 2 - self.zlo // 2, 3 - 3 * (self.zlo // 2)]
         self.far = {"zhi": 1 - self.zhi}
 
 
@@ -85,6 +88,28 @@
     def sent(self):
         for index in list(self.pushed):
             self.left(index)
+
+
+class Line:
+    def __init__(self, copies, at, region, x):
+        self.copies, self.at, self.region, self.x = copies, at, region, x
+        self.lands = [copies.reserve() for _ in range(3)]
+
+    def block(self, k):
+        return self.region(self.at.zsrc[k] * 4 + self.x)
+
+    def start(self):
+        block = self.block(0)
+        self.copies.push(block, block, {"zlo": self.at.zq}, self.lands[0])
+        self.copies.push(block, block, {"zlo": self.at.zi}, self.lands[1], self.at.inner)
+
+    def arrive(self, k):
+        block = self.block(k)
+        self.copies.got(self.lands[k - 1], block)
+        if k == 1:
+            self.copies.push(block, block, {"zlo": self.at.zi}, self.lands[2], self.at.inner)
+        else:
+            self.copies.push(block, block, {"zlo": self.at.zq}, self.lands[k - 1], self.at.inner)
 
 
 def greet(devices):
@@ -163,8 +188,7 @@
     z_steps = (1, 7, 2, 6, 3, 5, 4)
     deep_to = [lax.rem(deep + k, 8) for k in z_steps]
     order = [deep] + [lax.rem(deep + 8 - k, 8) for k in z_steps]
-    zs = [lax.rem(at.zlo + k, 4) for k in (1, 3, 2)]
-    zfrom = [at.zlo] + [lax.rem(at.zlo + 4 - k, 4) for k in (1, 3, 2)]
+    zsrc = at.zsrc
     peers = [(c, z, y) for z in (1, 0) for y in range(4) for c in (0, 1) if (c, z, y) != (0, 0, 0)]
     halves = (0, 1)
 
@@ -201,8 +225,8 @@
     def wo_block(chip):
         return wo_here.at[pl.ds(2 * at.y, 2), chip, at.core]
 
-    def wo_plane(y, core):
-        return wo_here.at[pl.ds(2 * y, 2), :, core]
+    def wo_plane(y, core, k):
+        return wo_here.at[pl.ds(2 * y, 2), aligned(zsrc[k], 4), core]
 
     def kv_block(chip):
         return kv.at[chip]
@@ -239,7 +263,8 @@
     for i in range(3):
         w_own[i].wait()
         copies.got(w_pair[i], wq_piece(1 - at.core, i))
-    w_z = [copies.push(wq_block(at.chip), wq_block(at.chip), {"zlo": z}) for z in zs]
+    w_line = Line(copies, at, wq_block, at.x)
+    w_line.start()
     w_x = [x_start(copies, at, wq_block, at.zlo)]
     far.append(copies.push(source[0], piece(at.share, 0), at.far))
     far.append(copies.push(source[1], piece(at.share, 1), at.far))
@@ -265,11 +290,11 @@
     w_f = []
 
     def w_open(k):
-        copies.got(w_z[k - 1], wq_block(zfrom[k] * 4 + at.x))
-        w_x.append(x_start(copies, at, wq_block, zfrom[k]))
+        w_line.arrive(k)
+        w_x.append(x_start(copies, at, wq_block, zsrc[k]))
 
     def w_forward(k):
-        w_f.append(x_forward(copies, at, wq_block, zfrom[k], w_x[k]))
+        w_f.append(x_forward(copies, at, wq_block, zsrc[k], w_x[k]))
 
     fwd.append(pass_tokens(own_f[0], near_ring[0], 0))
     w_forward(0)
@@ -292,21 +317,56 @@
     share_out(far_share)
     o_own.wait()
     copies.got(o_far, wo_here.at[far_share, at.chip, at.core])
-    o_z = [copies.push(wo_block(at.chip), wo_block(at.chip), {"zlo": z}) for z in zs]
-    o_x = [x_start(copies, at, wo_block, at.zlo)]
+    o_line = Line(copies, at, wo_block, at.x)
+    o_line.start()
+    o_x, o_f = [x_start(copies, at, wo_block, at.zlo)], []
+
+    def o_open(k):
+        o_line.arrive(k)
+        o_x.append(x_start(copies, at, wo_block, zsrc[k]))
+
+    def o_forward(k):
+        o_f.append(x_forward(copies, at, wo_block, zsrc[k], o_x[k]))
+
+    o_y, o_fwd, o_over = {}, {}, {}
+
+    def o_spread(k):
+        x_rest(copies, at, wo_block, zsrc[k], o_x[k], o_f[k])
+        plane = wo_plane(at.y, at.core, k)
+        o_y[k] = [copies.push(plane, plane, {"y": y}) for y in (at.yf, at.yb)]
+        o_over[k] = [copies.push(plane, plane, at.partner)]
+
+    def o_relay(k):
+        plane = wo_plane(at.yb, at.core, k)
+        copies.got(o_y[k][0], plane)
+        o_fwd[k] = copies.push(plane, plane, {"y": at.yf})
+        o_over[k].append(copies.push(plane, plane, at.partner))
+        plane = wo_plane(at.yf, at.core, k)
+        copies.got(o_y[k][1], plane)
+        o_over[k].append(copies.push(plane, plane, at.partner))
+
+    def o_last(k):
+        plane = wo_plane(at.yo, at.core, k)
+        copies.got(o_fwd[k], plane)
+        o_over[k].append(copies.push(plane, plane, at.partner))
+
     fwd = []
     for h in halves:
         fwd.append(pass_tokens(far_f[h], far_ring[0], h))
     share_out(far_ring[0])
+    o_open(1)
     for h in halves:
         copies.got(far_b[h], piece(far_ring[1], h))
     share_out(far_ring[1])
-    o_f = [x_forward(copies, at, wo_block, at.zlo, o_x[0])]
+    o_forward(0)
+    o_open(2)
     for h in halves:
         copies.got(fwd[h], piece(far_ring[2], h))
     share_out(far_ring[2])
+    o_open(3)
     for k in range(4):
-        x_rest(copies, at, wq_block, zfrom[k], w_x[k], w_f[k])
+        x_rest(copies, at, wq_block, zsrc[k], w_x[k], w_f[k])
+    o_spread(0)
     for index, share in shared:
         copies.got(index, share_block(1 - at.core, share))
 
@@ -317,9 +377,6 @@
     px = px * at.x + (1 - px) * at.xp
     pxs = px + 1 - 2 * lax.rem(px, 2)
     held = at.zlo * 4 + px
-    inner = jnp.logical_or(at.zlo == 1, at.zlo == 2)
-    zi = 3 - at.zlo
-    zsrc = [at.zlo, at.zq, 2 - at.zlo // 2, 3 - 3 * (at.zlo // 2)]
     handed = [copies.reserve() for _ in range(3)]
     for t in range(2):
         part = pl.ds(512 * t, 512)
@@ -374,7 +431,7 @@
                 both, kv[chip, 1], preferred_element_type=F32
             )
 
-    lands = [copies.reserve() for _ in range(3)]
+    kv_line = Line(copies, at, kv_block, px)
     beside, columns_over, beside_over = [], [], []
 
     def column(k, x):
@@ -382,16 +439,11 @@
 
     def kv_open(k):
         block = column(k, px)
-        if k > 0:
-            copies.got(lands[k - 1], block)
+        if k == 0:
+            kv_line.start()
+        else:
+            kv_line.arrive(k)
         beside.append(copies.push(block, block, {"x": at.xs}))
-        if k == 0:
-            copies.push(block, block, {"zlo": at.zq}, lands[0])
-            copies.push(block, block, {"zlo": zi}, lands[1], inner)
-        if k == 1:
-            copies.push(block, block, {"zlo": zi}, lands[2], inner)
-        if k > 1:
-            copies.push(block, block, {"zlo": at.zq}, lands[k - 1], inner)
         columns_over.append(copies.push(block, block, at.partner))
 
     def kv_beside(k):
@@ -425,27 +477,23 @@
 
     kv_open(0)
     for k in (1, 2, 3):
-        copies.got(o_z[k - 1], wo_block(zfrom[k] * 4 + at.x))
-        o_x.append(x_start(copies, at, wo_block, zfrom[k]))
+        o_forward(k)
     copies.got(handed[2], queries)
     attend_column(0)
+    for k in (1, 2, 3):
+        o_spread(k)
     attend_column_over(0)
-    for k in (1, 2, 3):
-        o_f.append(x_forward(copies, at, wo_block, zfrom[k], o_x[k]))
+    o_relay(0)
     kv_open(1)
     kv_beside(0)
     attend_beside(0)
-    for k in range(4):
-        x_rest(copies, at, wo_block, zfrom[k], o_x[k], o_f[k])
-    plane = wo_plane(at.y, at.core)
-    wo_f = copies.push(plane, plane, {"y": at.yf})
-    wo_b = copies.push(plane, plane, {"y": at.yb})
-    wo_p = [copies.push(plane, plane, at.partner)]
     attend_column(1)
+    o_last(0)
     attend_column_over(1)
     attend_beside_over(0)
     kv_open(2)
     kv_beside(1)
+    o_relay(1)
     attend_beside(1)
     attend_column(2)
     attend_column_over(2)
@@ -456,20 +504,25 @@
     block = ud_block(deep, at.x)
     along_z = [copies.push(block, block, depth(z)) for z in deep_to]
     kv_beside(2)
+    o_relay(2)
+    o_last(1)
     attend_beside(2)
     attend_column(3)
     attend_column_over(3)
     attend_beside_over(2)
     kv_beside(3)
+    opened, forwarded, lumps = [x_push(deep)], [], []
+
+    def open_group(k):
+        copies.got(along_z[k - 1], ud_block(order[k], at.x))
+        opened.append(x_push(order[k]))
+
+    o_relay(3)
+    o_last(2)
     attend_beside(3)
+    for k in (1, 2):
+        open_group(k)
     attend_beside_over(3)
-    plane = wo_plane(at.yb, at.core)
-    copies.got(wo_f, plane)
-    wo_fwd = copies.push(plane, plane, {"y": at.yf})
-    wo_p.append(copies.push(plane, plane, at.partner))
-    plane = wo_plane(at.yf, at.core)
-    copies.got(wo_b, plane)
-    wo_p.append(copies.push(plane, plane, at.partner))
     for t in range(2):
         part_rows = slice(512 * t, 512 * t + 512)
         attn[t] = (
@@ -504,12 +557,6 @@
                 copies.hand(needed(goal), head_rows(head), device, native, base + role)
             else:
                 copies.push(needed(goal), head_rows(head), device, base + role)
-    opened, forwarded, lumps = [x_push(deep)], [], []
-
-    def open_group(k):
-        copies.got(along_z[k - 1], ud_block(order[k], at.x))
-        opened.append(x_push(order[k]))
-
     def forward_group(k):
         block = ud_block(order[k], at.xb)
         copies.got(opened[k][0], block)
@@ -524,19 +571,17 @@
     shift = 2 * at.share - 1 - first
     for r in (1, 4):
         window[r] = jnp.zeros(window.shape[1:], F32)
-    for k in (1, 2, 3):
-        open_group(k)
+    open_group(3)
     forward_group(0)
-    plane = wo_plane(at.yo, at.core)
-    copies.got(wo_fwd, plane)
-    wo_p.append(copies.push(plane, plane, at.partner))
+    o_last(3)
     for base, (z, y) in zip(arrivals, places):
         _, zhi, y_from = peer(0, z, y, -1)
         whose = 2 * (2 * y_from + zhi)
         copies.got(base, head_rows(whose + at.side))
         copies.got(base + 1, head_rows(whose + 1 - at.side))
-    for index, y in zip(wo_p, (at.y, at.yb, at.yf, at.yo)):
-        copies.got(index, wo_plane(y, 1 - at.core))
+    for k in range(4):
+        for index, y in zip(o_over[k], (at.y, at.yb, at.yf, at.yo)):
+            copies.got(index, wo_plane(y, 1 - at.core, k))
     for k in (4, 5):
         open_group(k)
     forward_group(1)
@@ -707,7 +752,7 @@
             pltpu.VMEM((256, width), BF),
         ]
         + [pltpu.VMEM((64, width), BF)] * 4
-        + scratch(224, 8),
+        + scratch(288, 8),
         compiler_params=remote(1, 60),
     )(
         frame_time,

time: 229 us -> 247 us (1.079)
  Pallas kernels: 222 us -> 240 us
    pallas_call x1, Pallas kernels: 222 us -> 240 us  [shards(): pl.pallas_call(layer_kernel, out_shape=shape(64, width), in_specs=[SMEM]...]
where the time goes in v4:
time: 247 us; the launch traced here: 243 us
  Pallas kernels  240 us (97%)
  local copies, waits for them, and re-layouts  3.07 us (1%)
    pallas_call x1, Pallas kernels, shards(): pl.pallas_call(layer_kernel, out_shape=shape(64, width), in_specs=[SMEM]...  240 us

profile of v4, /device:TPU:1, one launch (start us, length us, event | category | flops | bytes accessed | tf_op | source)
XLA Modules:
  0.0 243.3 jit_solution(14837662886884722684)
XLA Ops:
  0.0 1.3 reshape.10.gain
  1.3 240.0 %shard_map.82 = bf16[64,3072]{1,0:T(8,128)(2,1)} custom-call(s32[32]{0:T(128)} %times.1, bf16[64,3072]{1,0:T(8,128)(2,1)} %bitcast.5, bf16[3,96,256]{2,1,0:T(8,128)(2,1)} %wq.1, bf16[96,256]{1,0:T(8,128)(2,1)} %bitcast.7, bf16[96,384]{1,0:T(8,128)(2,1)} %up.1, bf16[96,384]{1,0:T(8,128)(2,1)} %bitcast.6, bf16[1,3072]{1,0:T(2,128)(2,1)} %reshape.10.gain, ...), custom_call_target="tpu_custom_call" | custom-call | tf_op jit(solution)/shard_map/pallas_call | solution.py:730
  241.3 1.8 copy.10
